TPU v7x, 256 devices: a whole 4x4x8 slice. The times are simulated.
256 devices in a mesh: head: 4 (over y), seq: 16 (over z, core), ctx: 4 (over x).
Axes of the slice: x: 4, y: 4, z: 8, core: 2. Of those that a mesh axis runs over, the one named last changes fastest.
Arguments:
- queries: bfloat16 [128, 256, 2048], P(('seq', 'ctx'), 'head'), may hold values from -96 to 96
- keys: bfloat16 [128, 256, 2048], P(('seq', 'ctx'), 'head'), may hold values from -6 to 6
- values: bfloat16 [128, 256, 2048], P(('seq', 'ctx'), 'head'), may hold values from -6 to 6
- cotangent: bfloat16 [128, 256, 2048], P(('seq', 'ctx'), 'head'), may hold values from -6 to 6
Outputs:
- attended: bfloat16 [128, 256, 2048], P(('seq', 'ctx'), 'head')
- grad_queries: bfloat16 [128, 256, 2048], P(('seq', 'ctx'), 'head')
- grad_keys: bfloat16 [128, 256, 2048], P(('seq', 'ctx'), 'head')
- grad_values: bfloat16 [128, 256, 2048], P(('seq', 'ctx'), 'head')
All inputs are finite; a program needn't handle non-finite values.
Results may differ from a plain program's by a relative error of at most 0.0075.
Values may be sent and summed in bfloat16 or wider, within the bound.
No kernel may reach another device: no remote copies, remote signals or barrier semaphores. Data moves between devices by JAX's collectives and lax.ppermute only.
A program may use at most 64 MiB of HBM per device.

v0:
```python
import math

import jax
import jax.numpy as jnp
import numpy as np
from jax import lax
from jax.sharding import PartitionSpec as P

HD = 128


def as_sent(value):
    return jax.tree.map(lambda a: a.astype(jnp.bfloat16) if a.dtype == jnp.float32 else a, value)


def shifted(block, axis, distance):
    devices = range(lax.axis_size(axis))
    route = [(i - distance, i) for i in devices if i - distance in devices]
    return lax.ppermute(block, axis, route)


def key_offsets(block_rows):
    counts = [block_rows, block_rows, block_rows // 2, block_rows // 2] + [block_rows // 4] * 4
    return np.repeat(np.arange(8), counts).astype(np.int32)


def allowed_mask(block_index, block_rows):
    offsets = jnp.asarray(key_offsets(block_rows))
    row_ids = jnp.arange(block_rows, dtype=jnp.int32)
    col_ids = jnp.arange(offsets.shape[0], dtype=jnp.int32)
    usable = block_index - offsets >= 0
    causal = (offsets != 0)[None, :] | (col_ids[None, :] <= row_ids[:, None])
    return usable[None, :] & causal


def pooled(source, factor):
    n_rows, features = source.shape
    return (
        source.astype(jnp.float32)
        .reshape(n_rows // factor, factor, features)
        .mean(axis=1)
        .astype(jnp.bfloat16)
    )


def pool_stack(stack, factor):
    count, rows, features = stack.shape
    return pooled(stack.reshape(count * rows, features), factor).reshape(
        count, rows // factor, features
    )


def unpooled(grads, factor):
    n_rows, features = grads.shape
    spread = jnp.broadcast_to(grads[:, None, :] * (1.0 / factor), (n_rows, factor, features))
    return spread.reshape(n_rows * factor, features)


def head_core(queries, cotangent, keyset, valset, allowed):
    score_scale = 1.0 / math.sqrt(queries.shape[1])
    scores = jnp.dot(queries, keyset.T, preferred_element_type=jnp.float32) * score_scale
    scores = jnp.where(allowed, scores, -1e30)
    row_max = jnp.max(scores, axis=1, keepdims=True)
    exp_scores = jnp.exp(scores - row_max)
    weights = (exp_scores / jnp.sum(exp_scores, axis=1, keepdims=True)).astype(jnp.bfloat16)
    output = jnp.dot(weights, valset, preferred_element_type=jnp.float32).astype(jnp.bfloat16)
    dweights = jnp.dot(cotangent, valset.T, preferred_element_type=jnp.float32)
    wfloat = weights.astype(jnp.float32)
    row_delta = jnp.sum(wfloat * dweights, axis=1, keepdims=True)
    dscores = (wfloat * (dweights - row_delta) * score_scale).astype(jnp.bfloat16)
    dquery = jnp.dot(dscores, keyset, preferred_element_type=jnp.float32).astype(jnp.bfloat16)
    dkeys = jnp.dot(dscores.T, queries, preferred_element_type=jnp.float32)
    dvals = jnp.dot(weights.T, cotangent, preferred_element_type=jnp.float32)
    return (output, dquery, dkeys, dvals)


def block_core(queries, cotangent, keyset, valset, allowed, head_dim):
    head_count = queries.shape[1] // head_dim

    def split_heads(source):
        return source.reshape(source.shape[0], head_count, head_dim).transpose(1, 0, 2)

    def join_heads(source):
        return source.transpose(1, 0, 2).reshape(source.shape[1], head_count * head_dim)

    def per_head(members):
        return head_core(members[0], members[1], members[2], members[3], allowed)

    results = lax.map(
        per_head,
        (split_heads(queries), split_heads(cotangent), split_heads(keyset), split_heads(valset)),
    )
    return tuple((join_heads(result) for result in results))


def add_pair(table, slot, first, second):
    if slot in table:
        table[slot] = (table[slot][0] + first, table[slot][1] + second)
    else:
        table[slot] = (first, second)


def shards(queries, keys, values, cotangent):
    moved = (
        lax.all_to_all(queries, "head", split_axis=2, concat_axis=1, tiled=True),
        lax.all_to_all(keys, "head", split_axis=2, concat_axis=1, tiled=True),
        lax.all_to_all(values, "head", split_axis=2, concat_axis=1, tiled=True),
        lax.all_to_all(cotangent, "head", split_axis=2, concat_axis=1, tiled=True),
    )
    own_queries = moved[0]
    own_keys = moved[1]
    own_values = moved[2]
    own_cotangent = moved[3]
    block_rows = own_queries.shape[1]
    half = block_rows // 2
    quarter = block_rows // 4
    mid_k = pool_stack(own_keys, 2)
    mid_v = pool_stack(own_values, 2)
    far_k = pool_stack(own_keys, 4)
    far_v = pool_stack(own_values, 4)
    device_index = lax.axis_index(("seq", "ctx"))

    def fetch(members, distance):
        return jax.tree.map(
            lambda part, own: part.astype(own.dtype),
            shifted(as_sent(members), ("seq", "ctx"), distance),
            members,
        )

    first = fetch((own_keys[1], own_values[1], mid_k, mid_v), 1)
    second = fetch((mid_k[1], mid_v[1], far_k, far_v), 2)
    third = fetch((far_k, far_v), 3)
    fourth = fetch((far_k[1], far_v[1]), 4)
    third_k = third[0]
    third_v = third[1]
    fine_slots = {7: (first[0], first[1]), 8: (own_keys[0], own_values[0])}
    mid_slots = {
        5: (second[0], second[1]),
        6: (first[2][0], first[3][0]),
        7: (first[2][1], first[3][1]),
    }
    far_slots = {
        1: (fourth[0], fourth[1]),
        2: (third_k[0], third_v[0]),
        3: (third_k[1], third_v[1]),
        4: (second[2][0], second[3][0]),
        5: (second[2][1], second[3][1]),
    }
    base = 2 * block_rows
    farbase = 3 * block_rows
    gfine = {}
    gmid = {}
    gfar = {}
    outputs = []
    dqueries = []
    for local in range(2):
        pieces = [
            (own_keys[local], own_values[local]),
            fine_slots[7 + local],
            mid_slots[6 + local],
            mid_slots[5 + local],
        ]
        pieces = pieces + [far_slots[4 + local - step] for step in range(4)]
        keyset = jnp.concatenate([piece[0] for piece in pieces], axis=0)
        valset = jnp.concatenate([piece[1] for piece in pieces], axis=0)
        allowed = allowed_mask(2 * device_index + local, block_rows)
        output, dquery, dkeyset, dvalset = block_core(
            own_queries[local], own_cotangent[local], keyset, valset, allowed, HD
        )
        outputs.append(output)
        dqueries.append(dquery)
        add_pair(gfine, 8 + local, dkeyset[:block_rows], dvalset[:block_rows])
        add_pair(gfine, 7 + local, dkeyset[block_rows:base], dvalset[block_rows:base])
        add_pair(gmid, 6 + local, dkeyset[base : base + half], dvalset[base : base + half])
        add_pair(gmid, 5 + local, dkeyset[base + half : farbase], dvalset[base + half : farbase])
        for step in range(4):
            start = farbase + step * quarter
            add_pair(
                gfar,
                4 + local - step,
                dkeyset[start : start + quarter],
                dvalset[start : start + quarter],
            )
    mid_pair_k = jnp.stack([gmid[6][0], gmid[7][0]])
    mid_pair_v = jnp.stack([gmid[6][1], gmid[7][1]])
    far_near_k = jnp.stack([gfar[4][0], gfar[5][0]])
    far_near_v = jnp.stack([gfar[4][1], gfar[5][1]])
    far_back_k = jnp.stack([gfar[2][0], gfar[3][0]])
    far_back_v = jnp.stack([gfar[2][1], gfar[3][1]])

    def give(members, distance):
        return shifted(members, ("seq", "ctx"), -distance)

    back_one = give((gfine[7][0], gfine[7][1], mid_pair_k, mid_pair_v), 1)
    back_two = give((gmid[5][0], gmid[5][1], far_near_k, far_near_v), 2)
    back_three = give((far_back_k, far_back_v), 3)
    back_four = give((gfar[1][0], gfar[1][1]), 4)
    far_recv_k = back_two[2] + back_three[0]
    far_recv_v = back_two[3] + back_three[1]
    mid_recv_k = jnp.stack([back_one[2][0], back_one[2][1] + back_two[0]])
    mid_recv_v = jnp.stack([back_one[3][0], back_one[3][1] + back_two[1]])
    far_recv_k = jnp.stack([far_recv_k[0], far_recv_k[1] + back_four[0]])
    far_recv_v = jnp.stack([far_recv_v[0], far_recv_v[1] + back_four[1]])
    grad_keys = []
    grad_values = []
    for local in range(2):
        total_k = (
            gfine[8 + local][0] + unpooled(mid_recv_k[local], 2) + unpooled(far_recv_k[local], 4)
        )
        total_v = (
            gfine[8 + local][1] + unpooled(mid_recv_v[local], 2) + unpooled(far_recv_v[local], 4)
        )
        if local == 1:
            total_k = total_k + back_one[0]
            total_v = total_v + back_one[1]
        grad_keys.append(total_k.astype(jnp.bfloat16))
        grad_values.append(total_v.astype(jnp.bfloat16))
    final = (
        lax.all_to_all(
            as_sent(jnp.stack(outputs)), "head", split_axis=1, concat_axis=2, tiled=True
        ),
        lax.all_to_all(
            as_sent(jnp.stack(dqueries)), "head", split_axis=1, concat_axis=2, tiled=True
        ),
        lax.all_to_all(jnp.stack(grad_keys), "head", split_axis=1, concat_axis=2, tiled=True),
        lax.all_to_all(jnp.stack(grad_values), "head", split_axis=1, concat_axis=2, tiled=True),
    )
    return (final[0], final[1], final[2], final[3])


def solution(mesh):
    in_specs = (
        P(("seq", "ctx"), "head", None),
        P(("seq", "ctx"), "head", None),
        P(("seq", "ctx"), "head", None),
        P(("seq", "ctx"), "head", None),
    )
    out_specs = (
        P(("seq", "ctx"), "head", None),
        P(("seq", "ctx"), "head", None),
        P(("seq", "ctx"), "head", None),
        P(("seq", "ctx"), "head", None),
    )
    return jax.shard_map(shards, mesh=mesh, in_specs=in_specs, out_specs=out_specs, check_vma=False)
```

profile of v0, /device:TPU:102, one launch (start us, length us, event | category | flops | bytes accessed | tf_op | source)
XLA Modules:
  0.0 385.0 jit_solution(10847080513130878527)
XLA Ops:
  4.6 4.6 %all-to-all-start.2 = ((bf16[4,2,32768]{2,1,0:T(2,128)(2,1)}), bf16[4,2,32768]{2,1,0:T(2,128)(2,1)S(1)}, u32[]{:S(2)}, u32[]{:S(2)}) async-start(bf16[4,2,32768]{2,1,0:T(2,128)(2,1)} %reshape.496), calls=%async_computation.2 | async-start | bytes 1048576 | tf_op jit(solution)/shard_map/all_to_all | solution.py:107
  18.7 3.5 all-to-all-start.1
  30.1 5.5 %collective-permute-start.10 = (bf16[2,64,512]{2,1,0:T(8,128)(2,1)}, bf16[2,64,512]{2,1,0:T(8,128)(2,1)}, u32[]{:S(2)}, u32[]{:S(2)}) collective-permute-start(bf16[2,64,512]{2,1,0:T(8,128)(2,1)} %bitcast.19), channel_id=1, source_target_pairs={{0,3},{1,4},{2,5},{3,6},{4,7},{5,8},{6,9},{7,10},{8,11},{9,12},{10... | collective-permute-start | bytes 393224 | tf_op jit(solution)/shard_map/ppermute | solution.py:19
  37.3 4.7 %all-to-all-start = ((bf16[4,2,32768]{2,1,0:T(2,128)(2,1)}), bf16[4,2,32768]{2,1,0:T(2,128)(2,1)}, u32[]{:S(2)}, u32[]{:S(2)}) async-start(bf16[4,2,32768]{2,1,0:T(2,128)(2,1)} %reshape.492), calls=%async_computation | async-start | bytes 1048576 | tf_op jit(solution)/shard_map/all_to_all | solution.py:105
  56.4 5.1 %collective-permute-start.3 = (bf16[2,64,512]{2,1,0:T(8,128)(2,1)S(1)}, bf16[2,64,512]{2,1,0:T(8,128)(2,1)}, u32[]{:S(2)}, u32[]{:S(2)}) collective-permute-start(bf16[2,64,512]{2,1,0:T(8,128)(2,1)S(1)} %bitcast.404), channel_id=1, source_target_pairs={{0,2},{1,3},{2,4},{3,5},{4,6},{5,7},{6,8},{7,9},{8,10},{9,11},{10,... | collective-permute-start | bytes 393224 | tf_op jit(solution)/shard_map/ppermute | solution.py:19
  62.7 4.5 %all-to-all-start.3 = ((bf16[4,2,32768]{2,1,0:T(2,128)(2,1)}), bf16[4,2,32768]{2,1,0:T(2,128)(2,1)S(1)}, u32[]{:S(2)}, u32[]{:S(2)}) async-start(bf16[4,2,32768]{2,1,0:T(2,128)(2,1)} %reshape.498), calls=%async_computation.3 | async-start | bytes 1048576 | tf_op jit(solution)/shard_map/all_to_all | solution.py:108
  86.4 4.3 %collective-permute-start.7 = (bf16[2,128,512]{1,2,0:T(8,128)(2,1)}, bf16[2,128,512]{1,2,0:T(8,128)(2,1)S(1)}, u32[]{:S(2)}, u32[]{:S(2)}) collective-permute-start(bf16[2,128,512]{1,2,0:T(8,128)(2,1)} %copy.234), channel_id=1, source_target_pairs={{0,1},{1,2},{2,3},{3,4},{4,5},{5,6},{6,7},{7,8},{8,9},{9,10},{10,1... | collective-permute-start | bytes 786440 | tf_op jit(solution)/shard_map/ppermute | solution.py:19
  94.9 3.5 collective-permute-start.8
  99.4 5.5 %collective-permute-start.1 = (bf16[2,128,512]{2,1,0:T(8,128)(2,1)}, bf16[2,128,512]{2,1,0:T(8,128)(2,1)}, u32[]{:S(2)}, u32[]{:S(2)}) collective-permute-start(bf16[2,128,512]{2,1,0:T(8,128)(2,1)} %bitcast.391), channel_id=1, source_target_pairs={{0,1},{1,2},{2,3},{3,4},{4,5},{5,6},{6,7},{7,8},{8,9},{9,10},{10,1... | collective-permute-start | bytes 786440 | tf_op jit(solution)/shard_map/ppermute | solution.py:19
  145.6 32.2 %while.34 = (s32[]{:T(128)}, bf16[4,256,128]{1,2,0:T(8,128)(2,1)}, bf16[4,256,128]{1,2,0:T(8,128)(2,1)}, f32[4,1024,128]{1,2,0:T(8,128)S(1)}, f32[4,1024,128]{1,...) while((s32[]{:T(128)}, bf16[4,256,128]{1,2,0:T(8,128)(2,1)}, ...), condition=%wide.region_8.9_spmd.clone, body=%wide.region_4.8_spmd.clone.sunk | while | flops 407698688 | bytes 12991121 | solution.py:89
  177.8 3.2 copy.253
  185.5 35.5 %while.35 = (s32[]{:T(128)}, bf16[4,256,128]{1,2,0:T(8,128)(2,1)}, bf16[4,256,128]{1,2,0:T(8,128)(2,1)}, f32[4,1024,128]{1,2,0:T(8,128)S(1)}, f32[4,1024,128]{1,...) while((s32[]{:T(128)}, bf16[4,256,128]{1,2,0:T(8,128)(2,1)}, ...), condition=%wide.region_13.14_spmd.clone, body=%wide.region_9.13_spmd.clone.sunk | while | flops 407698688 | bytes 11942517 | solution.py:89
  235.6 5.1 %collective-permute-start.20 = (f32[2,64,512]{2,1,0:T(8,128)}, f32[2,64,512]{2,1,0:T(8,128)}, u32[]{:S(2)}, u32[]{:S(2)}) collective-permute-start(f32[2,64,512]{2,1,0:T(8,128)} %pad_maximum_fusion.9), channel_id=1, source_target_pairs={{3,0},{4,1},{5,2},{6,3},{7,4},{8,5},{9,6},{10,7},{11,8},{12,9},{13... | collective-permute-start | bytes 786440 | tf_op jit(solution)/shard_map/ppermute | solution.py:19
  251.3 4.5 %collective-permute-start.14 = (f32[2,64,512]{2,1,0:T(8,128)}, f32[2,64,512]{2,1,0:T(8,128)}, u32[]{:S(2)}, u32[]{:S(2)}) collective-permute-start(f32[2,64,512]{2,1,0:T(8,128)} %pad_maximum_fusion.7), channel_id=1, source_target_pairs={{3,0},{4,1},{5,2},{6,3},{7,4},{8,5},{9,6},{10,7},{11,8},{12,9},{13... | collective-permute-start | bytes 786440 | tf_op jit(solution)/shard_map/ppermute | solution.py:19
  261.9 3.6 all-to-all-start.5
  272.2 3.1 collective-permute-start.21
  286.9 4.1 %collective-permute-start.15 = (f32[128,512]{0,1:T(8,128)}, f32[128,512]{0,1:T(8,128)}, u32[]{:S(2)}, u32[]{:S(2)}) collective-permute-start(f32[128,512]{0,1:T(8,128)} %bitcast.55), channel_id=1, source_target_pairs={{2,0},{3,1},{4,2},{5,3},{6,4},{7,5},{8,6},{9,7},{10,8},{11,9},{12,... | collective-permute-start | bytes 786440 | tf_op jit(solution)/shard_map/ppermute | solution.py:19
  296.5 18.2 %collective-permute-start.17 = (f32[256,512]{0,1:T(8,128)}, f32[256,512]{0,1:T(8,128)}, u32[]{:S(2)}, u32[]{:S(2)}) collective-permute-start(f32[256,512]{0,1:T(8,128)} %bitcast.392), channel_id=1, source_target_pairs={{1,0},{2,1},{3,2},{4,3},{5,4},{6,5},{7,6},{8,7},{9,8},{10,9},{11,1... | collective-permute-start | bytes 1572872 | tf_op jit(solution)/shard_map/ppermute | solution.py:19
  316.5 6.8 %collective-permute-done.15 = f32[128,512]{0,1:T(8,128)} collective-permute-done((f32[128,512]{0,1:T(8,128)}, f32[128,512]{0,1:T(8,128)}, u32[]{:S(2)}, u32[]{:S(2)}) %collective-permute-start.15) | collective-permute-done | bytes 262176 | tf_op jit(solution)/shard_map/ppermute | solution.py:19
  339.2 4.9 %all-to-all-start.4 = ((bf16[2,256,512]{2,0,1:T(2,128)(2,1)}), bf16[2,256,512]{2,0,1:T(2,128)(2,1)S(1)}, u32[]{:S(2)}, u32[]{:S(2)}) async-start(bf16[2,256,512]{2,0,1:T(2,128)(2,1)} %copy.256), calls=%async_computation.4 | async-start | bytes 1048576 | tf_op jit(solution)/shard_map/all_to_all | solution.py:219
  357.7 4.8 %all-to-all-start.7 = ((bf16[2,256,512]{2,0,1:T(2,128)(2,1)}), bf16[2,256,512]{2,0,1:T(2,128)(2,1)S(1)}, u32[]{:S(2)}, u32[]{:S(2)}) async-start(bf16[2,256,512]{2,0,1:T(2,128)(2,1)} %copy.293), calls=%async_computation.7 | async-start | bytes 1048576 | tf_op jit(solution)/shard_map/all_to_all | solution.py:226
  363.8 8.7 %all-to-all-done.7 = bf16[2,256,512]{2,0,1:T(2,128)(2,1)S(1)} async-done(((bf16[2,256,512]{2,0,1:T(2,128)(2,1)}), bf16[2,256,512]{2,0,1:T(2,128)(2,1)S(1)}, u32[]{:S(2)}, u32[]{:S(2)}) %all-to-all-start.7) | async-done | bytes 524320 | tf_op jit(solution)/shard_map/all_to_all | solution.py:226
  372.5 3.5 all-to-all-start.6
  378.7 5.3 %all-to-all-done.6 = bf16[2,256,512]{2,0,1:T(2,128)(2,1)S(1)} async-done(((bf16[2,256,512]{2,0,1:T(2,128)(2,1)}), bf16[2,256,512]{2,0,1:T(2,128)(2,1)S(1)}, u32[]{:S(2)}, u32[]{:S(2)}) %all-to-all-start.6) | async-done | bytes 524320 | tf_op jit(solution)/shard_map/all_to_all | solution.py:225
  (408 shorter events, 265.7 us)
Async XLA Ops:
  28.2 63.9 %collective-permute-start.9 = (bf16[2,64,512]{2,1,0:T(8,128)(2,1)}, bf16[2,64,512]{2,1,0:T(8,128)(2,1)}, u32[]{:S(2)}, u32[]{:S(2)}) collective-permute-start(bf16[2,64,512]{2,1,0:T(8,128)(2,1)} %bitcast.19), channel_id=1, source_target_pairs={{0,2},{1,3},{2,4},{3,5},{4,6},{5,7},{6,8},{7,9},{8,10},{9,11},{10,... | collective-permute-start | bytes 393224 | tf_op jit(solution)/shard_map/ppermute | solution.py:19
  30.1 64.8 %collective-permute-start.10 = (bf16[2,64,512]{2,1,0:T(8,128)(2,1)}, bf16[2,64,512]{2,1,0:T(8,128)(2,1)}, u32[]{:S(2)}, u32[]{:S(2)}) collective-permute-start(bf16[2,64,512]{2,1,0:T(8,128)(2,1)} %bitcast.19), channel_id=1, source_target_pairs={{0,3},{1,4},{2,5},{3,6},{4,7},{5,8},{6,9},{7,10},{8,11},{9,12},{10... | collective-permute-start | bytes 393224 | tf_op jit(solution)/shard_map/ppermute | solution.py:19
  37.3 25.4 %all-to-all-start = ((bf16[4,2,32768]{2,1,0:T(2,128)(2,1)}), bf16[4,2,32768]{2,1,0:T(2,128)(2,1)}, u32[]{:S(2)}, u32[]{:S(2)}) async-start(bf16[4,2,32768]{2,1,0:T(2,128)(2,1)} %reshape.492), calls=%async_computation | async-start | bytes 1048576 | tf_op jit(solution)/shard_map/all_to_all | solution.py:105
  51.3 31.7 %collective-permute-start.11 = (bf16[64,512]{1,0:T(8,128)(2,1)S(1)}, bf16[64,512]{1,0:T(8,128)(2,1)}, u32[]{:S(2)}, u32[]{:S(2)}) collective-permute-start(bf16[64,512]{1,0:T(8,128)(2,1)S(1)} %slice.344), channel_id=1, source_target_pairs={{0,4},{1,5},{2,6},{3,7},{4,8},{5,9},{6,10},{7,11},{8,12},{9,13},{1... | collective-permute-start | bytes 196616 | tf_op jit(solution)/shard_map/ppermute | solution.py:19
  56.4 42.9 %collective-permute-start.3 = (bf16[2,64,512]{2,1,0:T(8,128)(2,1)S(1)}, bf16[2,64,512]{2,1,0:T(8,128)(2,1)}, u32[]{:S(2)}, u32[]{:S(2)}) collective-permute-start(bf16[2,64,512]{2,1,0:T(8,128)(2,1)S(1)} %bitcast.404), channel_id=1, source_target_pairs={{0,2},{1,3},{2,4},{3,5},{4,6},{5,7},{6,8},{7,9},{8,10},{9,11},{10,... | collective-permute-start | bytes 393224 | tf_op jit(solution)/shard_map/ppermute | solution.py:19
  68.0 18.4 %collective-permute-start.5 = (bf16[64,512]{1,0:T(8,128)(2,1)}, bf16[64,512]{1,0:T(8,128)(2,1)}, u32[]{:S(2)}, u32[]{:S(2)}) collective-permute-start(bf16[64,512]{1,0:T(8,128)(2,1)} %slice.336), channel_id=1, source_target_pairs={{0,4},{1,5},{2,6},{3,7},{4,8},{5,9},{6,10},{7,11},{8,12},{9,13},{1... | collective-permute-start | bytes 196616 | tf_op jit(solution)/shard_map/ppermute | solution.py:19
  83.0 22.7 %collective-permute-start.4 = (bf16[2,64,512]{2,1,0:T(8,128)(2,1)S(1)}, bf16[2,64,512]{2,1,0:T(8,128)(2,1)}, u32[]{:S(2)}, u32[]{:S(2)}) collective-permute-start(bf16[2,64,512]{2,1,0:T(8,128)(2,1)S(1)} %bitcast.405), channel_id=1, source_target_pairs={{0,3},{1,4},{2,5},{3,6},{4,7},{5,8},{6,9},{7,10},{8,11},{9,12},{10... | collective-permute-start | bytes 393224 | tf_op jit(solution)/shard_map/ppermute | solution.py:19
  86.4 33.3 %collective-permute-start.7 = (bf16[2,128,512]{1,2,0:T(8,128)(2,1)}, bf16[2,128,512]{1,2,0:T(8,128)(2,1)S(1)}, u32[]{:S(2)}, u32[]{:S(2)}) collective-permute-start(bf16[2,128,512]{1,2,0:T(8,128)(2,1)} %copy.234), channel_id=1, source_target_pairs={{0,1},{1,2},{2,3},{3,4},{4,5},{5,6},{6,7},{7,8},{8,9},{9,10},{10,1... | collective-permute-start | bytes 786440 | tf_op jit(solution)/shard_map/ppermute | solution.py:19
  92.1 29.0 %collective-permute-start.6 = (bf16[256,512]{1,0:T(8,128)(2,1)}, bf16[256,512]{1,0:T(8,128)(2,1)}, u32[]{:S(2)}, u32[]{:S(2)}) collective-permute-start(bf16[256,512]{1,0:T(8,128)(2,1)} %bitcast.376), channel_id=1, source_target_pairs={{0,1},{1,2},{2,3},{3,4},{4,5},{5,6},{6,7},{7,8},{8,9},{9,10},{10,1... | collective-permute-start | bytes 786440 | tf_op jit(solution)/shard_map/ppermute | solution.py:19
  99.4 34.6 %collective-permute-start.1 = (bf16[2,128,512]{2,1,0:T(8,128)(2,1)}, bf16[2,128,512]{2,1,0:T(8,128)(2,1)}, u32[]{:S(2)}, u32[]{:S(2)}) collective-permute-start(bf16[2,128,512]{2,1,0:T(8,128)(2,1)} %bitcast.391), channel_id=1, source_target_pairs={{0,1},{1,2},{2,3},{3,4},{4,5},{5,6},{6,7},{7,8},{8,9},{9,10},{10,1... | collective-permute-start | bytes 786440 | tf_op jit(solution)/shard_map/ppermute | solution.py:19
  109.8 25.5 %collective-permute-start = (bf16[256,512]{1,0:T(8,128)(2,1)}, bf16[256,512]{1,0:T(8,128)(2,1)}, u32[]{:S(2)}, u32[]{:S(2)}) collective-permute-start(bf16[256,512]{1,0:T(8,128)(2,1)} %bitcast.375), channel_id=1, source_target_pairs={{0,1},{1,2},{2,3},{3,4},{4,5},{5,6},{6,7},{7,8},{8,9},{9,10},{10,1... | collective-permute-start | bytes 786440 | tf_op jit(solution)/shard_map/ppermute | solution.py:19
  235.6 33.8 %collective-permute-start.20 = (f32[2,64,512]{2,1,0:T(8,128)}, f32[2,64,512]{2,1,0:T(8,128)}, u32[]{:S(2)}, u32[]{:S(2)}) collective-permute-start(f32[2,64,512]{2,1,0:T(8,128)} %pad_maximum_fusion.9), channel_id=1, source_target_pairs={{3,0},{4,1},{5,2},{6,3},{7,4},{8,5},{9,6},{10,7},{11,8},{12,9},{13... | collective-permute-start | bytes 786440 | tf_op jit(solution)/shard_map/ppermute | solution.py:19
  245.2 26.9 %collective-permute-start.19 = (f32[2,64,512]{2,1,0:T(8,128)}, f32[2,64,512]{2,1,0:T(8,128)}, u32[]{:S(2)}, u32[]{:S(2)}) collective-permute-start(f32[2,64,512]{2,1,0:T(8,128)} %pad_maximum_fusion.8), channel_id=1, source_target_pairs={{2,0},{3,1},{4,2},{5,3},{6,4},{7,5},{8,6},{9,7},{10,8},{11,9},{12,... | collective-permute-start | bytes 786440 | tf_op jit(solution)/shard_map/ppermute | solution.py:19
  247.9 34.5 %collective-permute-start.22 = (f32[64,512]{1,0:T(8,128)}, f32[64,512]{1,0:T(8,128)S(1)}, u32[]{:S(2)}, u32[]{:S(2)}) collective-permute-start(f32[64,512]{1,0:T(8,128)} %copy.309), channel_id=1, source_target_pairs={{4,0},{5,1},{6,2},{7,3},{8,4},{9,5},{10,6},{11,7},{12,8},{13,9},{1... | collective-permute-start | bytes 393224 | tf_op jit(solution)/shard_map/ppermute | solution.py:19
  251.3 25.1 %collective-permute-start.14 = (f32[2,64,512]{2,1,0:T(8,128)}, f32[2,64,512]{2,1,0:T(8,128)}, u32[]{:S(2)}, u32[]{:S(2)}) collective-permute-start(f32[2,64,512]{2,1,0:T(8,128)} %pad_maximum_fusion.7), channel_id=1, source_target_pairs={{3,0},{4,1},{5,2},{6,3},{7,4},{8,5},{9,6},{10,7},{11,8},{12,9},{13... | collective-permute-start | bytes 786440 | tf_op jit(solution)/shard_map/ppermute | solution.py:19
  256.8 22.7 %collective-permute-start.13 = (f32[2,64,512]{2,1,0:T(8,128)}, f32[2,64,512]{2,1,0:T(8,128)}, u32[]{:S(2)}, u32[]{:S(2)}) collective-permute-start(f32[2,64,512]{2,1,0:T(8,128)} %pad_maximum_fusion.6), channel_id=1, source_target_pairs={{2,0},{3,1},{4,2},{5,3},{6,4},{7,5},{8,6},{9,7},{10,8},{11,9},{12,... | collective-permute-start | bytes 786440 | tf_op jit(solution)/shard_map/ppermute | solution.py:19
  261.9 77.3 %all-to-all-start.5 = ((bf16[2,256,512]{2,0,1:T(2,128)(2,1)}), bf16[2,256,512]{2,0,1:T(2,128)(2,1)S(1)}, u32[]{:S(2)}, u32[]{:S(2)}) async-start(bf16[2,256,512]{2,0,1:T(2,128)(2,1)} %copy.261), calls=%async_computation.5 | async-start | bytes 1048576 | tf_op jit(solution)/shard_map/all_to_all | solution.py:222
  269.4 45.3 %collective-permute-start.18 = (f32[2,128,512]{1,2,0:T(8,128)}, f32[2,128,512]{1,2,0:T(8,128)}, u32[]{:S(2)}, u32[]{:S(2)}) collective-permute-start(f32[2,128,512]{1,2,0:T(8,128)} %pad_maximum_fusion.4), channel_id=1, source_target_pairs={{1,0},{2,1},{3,2},{4,3},{5,4},{6,5},{7,6},{8,7},{9,8},{10,9},{11,1... | collective-permute-start | bytes 1572872 | tf_op jit(solution)/shard_map/ppermute | solution.py:19
  272.2 24.4 %collective-permute-start.21 = (f32[128,512]{0,1:T(8,128)}, f32[128,512]{0,1:T(8,128)}, u32[]{:S(2)}, u32[]{:S(2)}) collective-permute-start(f32[128,512]{0,1:T(8,128)} %bitcast.75), channel_id=1, source_target_pairs={{2,0},{3,1},{4,2},{5,3},{6,4},{7,5},{8,6},{9,7},{10,8},{11,9},{12,... | collective-permute-start | bytes 786440 | tf_op jit(solution)/shard_map/ppermute | solution.py:19
  276.4 60.8 %collective-permute-start.23 = (f32[256,512]{0,1:T(8,128)}, f32[256,512]{0,1:T(8,128)}, u32[]{:S(2)}, u32[]{:S(2)}) collective-permute-start(f32[256,512]{0,1:T(8,128)} %bitcast.393), channel_id=1, source_target_pairs={{1,0},{2,1},{3,2},{4,3},{5,4},{6,5},{7,6},{8,7},{9,8},{10,9},{11,1... | collective-permute-start | bytes 1572872 | tf_op jit(solution)/shard_map/ppermute | solution.py:19
  279.5 46.9 %collective-permute-start.12 = (f32[2,128,512]{1,2,0:T(8,128)}, f32[2,128,512]{1,2,0:T(8,128)}, u32[]{:S(2)}, u32[]{:S(2)}) collective-permute-start(f32[2,128,512]{1,2,0:T(8,128)} %pad_maximum_fusion.2), channel_id=1, source_target_pairs={{1,0},{2,1},{3,2},{4,3},{5,4},{6,5},{7,6},{8,7},{9,8},{10,9},{11,1... | collective-permute-start | bytes 1572872 | tf_op jit(solution)/shard_map/ppermute | solution.py:19
  286.9 36.3 %collective-permute-start.15 = (f32[128,512]{0,1:T(8,128)}, f32[128,512]{0,1:T(8,128)}, u32[]{:S(2)}, u32[]{:S(2)}) collective-permute-start(f32[128,512]{0,1:T(8,128)} %bitcast.55), channel_id=1, source_target_pairs={{2,0},{3,1},{4,2},{5,3},{6,4},{7,5},{8,6},{9,7},{10,8},{11,9},{12,... | collective-permute-start | bytes 786440 | tf_op jit(solution)/shard_map/ppermute | solution.py:19
  296.5 59.6 %collective-permute-start.17 = (f32[256,512]{0,1:T(8,128)}, f32[256,512]{0,1:T(8,128)}, u32[]{:S(2)}, u32[]{:S(2)}) collective-permute-start(f32[256,512]{0,1:T(8,128)} %bitcast.392), channel_id=1, source_target_pairs={{1,0},{2,1},{3,2},{4,3},{5,4},{6,5},{7,6},{8,7},{9,8},{10,9},{11,1... | collective-permute-start | bytes 1572872 | tf_op jit(solution)/shard_map/ppermute | solution.py:19
  339.2 18.5 %all-to-all-start.4 = ((bf16[2,256,512]{2,0,1:T(2,128)(2,1)}), bf16[2,256,512]{2,0,1:T(2,128)(2,1)S(1)}, u32[]{:S(2)}, u32[]{:S(2)}) async-start(bf16[2,256,512]{2,0,1:T(2,128)(2,1)} %copy.256), calls=%async_computation.4 | async-start | bytes 1048576 | tf_op jit(solution)/shard_map/all_to_all | solution.py:219
  (49 other events, 423.3 us)
where the time goes:
time: 389 us; the launch traced here: 385 us
  local copies, waits for them, and re-layouts  128 us (33%)
  starting transfers between devices  125 us (32%)
  matrix products  56 us (14%)
  other arithmetic  41.6 us (11%)
  waiting for transfers between devices  31.9 us (8%)
    ppermute x24, starting transfers between devices, shifted(): return lax.ppermute(block, axis, route)  91.3 us
    unnamed x114, local copies, waits for them, and re-layouts  40.9 us
    reshape x16, local copies, waits for them, and re-layouts, unpooled(): return spread.reshape(n_rows * factor, features)  14.6 us
    ppermute x24, waiting for transfers between devices, shifted(): return lax.ppermute(block, axis, route)  12.4 us
    dot_general x8, matrix products, head_core(): dvals = jnp.dot(weights.T, cotangent, preferred_element_type=jnp.float32)  12 us
    add x6, other arithmetic, add_pair(): table[slot] = (table[slot][0] + first, table[slot][1] + second)  11.6 us
    dot_general x8, matrix products, head_core(): dweights = jnp.dot(cotangent, valset.T, preferred_element_type=jnp.float32)  11.2 us
    dot_general x8, matrix products, head_core(): jnp.dot(queries, keyset.T, preferred_element_type=jnp.float32) * score_scale  10.8 us
  transfers between devices with their start and end apart: 32, of which 7 were waited for; matrix products, arithmetic and copies ran while one was open for 31% of the time, Pallas kernels for 0%

commit v1 on v0

v1 whole, which is shorter than its diff:
```python
import functools
import math

import jax
import jax.numpy as jnp
from jax import lax
from jax.experimental import pallas as pl
from jax.experimental.pallas import tpu as pltpu
from jax.sharding import PartitionSpec as P

HD = 128
BLOCK = 256
HALF = BLOCK // 2
QUARTER = BLOCK // 4
SCALE = 1.0 / math.sqrt(HD)
LOG2E = 1.0 / math.log(2.0)
NEG = -1e30
HALO_FINE = BLOCK
HALO_MID = 2 * HALF
HALO_FAR = 6 * QUARTER
HALO = HALO_FINE + HALO_MID + HALO_FAR
BACK = BLOCK + 2 * HALF + 4 * QUARTER
GROUP_AXES = ("ctx", "head")
VMEM = 48 * 1024 * 1024


def whole(count):
    return [pl.BlockSpec(memory_space=pltpu.VMEM)] * count


def params():
    return pltpu.CompilerParams(vmem_limit_bytes=VMEM)


def cost(flops, nbytes):
    return pl.CostEstimate(flops=flops, bytes_accessed=nbytes, transcendentals=0)


def spread_body(first, second, out):
    for head in range(out.shape[0]):
        out[head, 0] = first[:, :, head * HD : (head + 1) * HD]
        out[head, 1] = second[:, :, head * HD : (head + 1) * HD]


def spread(first, second):
    blocks, rows, features = first.shape
    heads = features // HD
    return pl.pallas_call(
        spread_body,
        out_shape=jax.ShapeDtypeStruct((heads, 2, blocks, rows, HD), first.dtype),
        in_specs=whole(2),
        out_specs=whole(1)[0],
        compiler_params=params(),
        cost_estimate=cost(0, 4 * first.size * 2),
    )(first, second)


def join_body(moved, first, second):
    for head in range(moved.shape[0]):
        first[:, :, head * HD : (head + 1) * HD] = moved[head, 0]
        second[:, :, head * HD : (head + 1) * HD] = moved[head, 1]


def join(moved):
    heads, _, blocks, rows, _ = moved.shape
    out = jax.ShapeDtypeStruct((blocks, rows, heads * HD), moved.dtype)
    return pl.pallas_call(
        join_body,
        out_shape=(out, out),
        in_specs=whole(1),
        out_specs=tuple(whole(2)),
        compiler_params=params(),
        cost_estimate=cost(0, 2 * moved.size * 2),
    )(moved)


def pool_matrix():
    row = lax.broadcasted_iota(jnp.int32, (HALF + QUARTER, BLOCK), 0)
    col = lax.broadcasted_iota(jnp.int32, (HALF + QUARTER, BLOCK), 1)
    pair = (row < HALF) & ((col >> 1) == row)
    four = (row >= HALF) & ((col >> 2) == row - HALF)
    both = jnp.where(pair, 0.5, 0.0) + jnp.where(four, 0.25, 0.0)
    return both.astype(jnp.bfloat16)


def pool_body(moved, fine, mid, far, msg):
    sources, _, local, rows, _ = moved.shape
    per_block = BLOCK // rows
    blocks = sources // per_block * local
    matrix = pool_matrix()
    for kv in range(2):
        for block in range(blocks):
            first = block // local * per_block
            tokens = jnp.concatenate(
                [moved[first + part, kv, block % local] for part in range(per_block)], axis=0
            )
            pooled = jnp.dot(matrix, tokens, preferred_element_type=jnp.float32)
            pooled = pooled.astype(jnp.bfloat16)
            fine[kv, block * BLOCK : (block + 1) * BLOCK] = tokens
            mid[kv, block * HALF : (block + 1) * HALF] = pooled[:HALF]
            far[kv, block * QUARTER : (block + 1) * QUARTER] = pooled[HALF:]
            from_end = blocks - block
            if from_end == 1:
                msg[kv, :HALO_FINE] = tokens
            if from_end in (2, 3):
                start = HALO_FINE + (3 - from_end) * HALF
                msg[kv, start : start + HALF] = pooled[:HALF]
            if 2 <= from_end <= 7:
                start = HALO_FINE + HALO_MID + (7 - from_end) * QUARTER
                msg[kv, start : start + QUARTER] = pooled[HALF:]


def pool(moved):
    sources, _, local, rows, _ = moved.shape
    blocks = sources * rows // BLOCK * local
    shape = functools.partial(jax.ShapeDtypeStruct, dtype=jnp.bfloat16)
    return pl.pallas_call(
        pool_body,
        out_shape=(
            shape((2, blocks * BLOCK, HD)),
            shape((2, blocks * HALF, HD)),
            shape((2, blocks * QUARTER, HD)),
            shape((2, HALO, HD)),
        ),
        in_specs=whole(1),
        out_specs=tuple(whole(4)),
        compiler_params=params(),
        cost_estimate=cost(4 * blocks * 192 * BLOCK * HD, moved.size * 6),
    )(moved)


def dot_nt(a, b):
    return lax.dot_general(a, b, (((1,), (1,)), ((), ())), preferred_element_type=jnp.float32)


def dot_tn(a, b):
    return lax.dot_general(a, b, (((0,), (0,)), ((), ())), preferred_element_type=jnp.float32)


def dot_nn(a, b):
    return jnp.dot(a, b, preferred_element_type=jnp.float32)


def attend_body(
    first_group, moved, fine, mid, far, halo, out, total, back, fext, mext, rext, fgrad, mgrad, rgrad
):
    sources, _, local, rows, _ = moved.shape
    per_block = BLOCK // rows
    blocks = sources // per_block * local
    matrix = pool_matrix()
    for kv in range(2):
        tokens = halo[kv, :HALO_FINE]
        pooled = jnp.dot(matrix, tokens, preferred_element_type=jnp.float32).astype(jnp.bfloat16)
        fext[kv, :BLOCK] = tokens
        fext[kv, BLOCK:] = fine[kv]
        mext[kv, : 2 * HALF] = halo[kv, HALO_FINE : HALO_FINE + HALO_MID]
        mext[kv, 2 * HALF : 3 * HALF] = pooled[:HALF]
        mext[kv, 3 * HALF :] = mid[kv]
        rext[kv, : 6 * QUARTER] = halo[kv, HALO_FINE + HALO_MID :]
        rext[kv, 6 * QUARTER : 7 * QUARTER] = pooled[HALF:]
        rext[kv, 7 * QUARTER :] = far[kv]
    fgrad[...] = jnp.zeros_like(fgrad)
    mgrad[...] = jnp.zeros_like(mgrad)
    rgrad[...] = jnp.zeros_like(rgrad)
    is_first = first_group[0]

    def one_block(step, inner):
        block = step * local + inner
        fine_at = pl.ds(pl.multiple_of(block * BLOCK, BLOCK), 2 * BLOCK)
        mid_at = pl.ds(pl.multiple_of(block * HALF, HALF), 2 * HALF)
        far_at = pl.ds(pl.multiple_of(block * QUARTER, QUARTER), 4 * QUARTER)

        def window(kv):
            return jnp.concatenate([fext[kv, fine_at], mext[kv, mid_at], rext[kv, far_at]], axis=0)

        def chunk(which):
            return jnp.concatenate(
                [moved[step * per_block + part, which, inner] for part in range(per_block)], axis=0
            )

        queries = chunk(0)
        cotangent = chunk(1)
        keyset = window(0)
        valset = window(1)
        scores = dot_nt(keyset, queries)
        row = lax.broadcasted_iota(jnp.int32, (BLOCK, BLOCK), 0)
        col = lax.broadcasted_iota(jnp.int32, (BLOCK, BLOCK), 1)
        absent = is_first * jnp.maximum(1 - block, 0) * BLOCK
        absent_mid = is_first * jnp.maximum(3 - block, 0) * HALF
        absent_far = is_first * jnp.maximum(7 - block, 0) * QUARTER
        scores = jnp.concatenate(
            [
                jnp.where(row < absent, NEG, scores[:BLOCK]),
                jnp.where(row <= col, scores[BLOCK : 2 * BLOCK], NEG),
                jnp.where(row < absent_mid, NEG, scores[2 * BLOCK : 3 * BLOCK]),
                jnp.where(row < absent_far, NEG, scores[3 * BLOCK :]),
            ],
            axis=0,
        )
        factor = SCALE * LOG2E
        top = jnp.max(scores, axis=0, keepdims=True)
        powers = jnp.exp2((scores - top) * factor)
        norm = 1.0 / jnp.sum(powers, axis=0, keepdims=True)
        weights = powers * norm
        weights_low = weights.astype(jnp.bfloat16)
        attended = dot_tn(valset, weights_low)
        turned = jnp.transpose(cotangent.astype(jnp.float32))
        delta = jnp.sum(attended * turned, axis=0, keepdims=True)
        dweights = dot_nt(valset, cotangent)
        dscores = (weights * (dweights - delta)).astype(jnp.bfloat16)
        dqueries = dot_tn(keyset, dscores) * SCALE
        dkeys = dot_nn(dscores, queries) * SCALE
        dvalues = dot_nn(weights_low, cotangent)
        attended_rows = jnp.transpose(attended).astype(jnp.bfloat16)
        dqueries_rows = jnp.transpose(dqueries).astype(jnp.bfloat16)
        for part in range(per_block):
            at = slice(part * rows, (part + 1) * rows)
            out[step * per_block + part, 0, inner] = attended_rows[at]
            out[step * per_block + part, 1, inner] = dqueries_rows[at]
        for kv, grads in enumerate((dkeys, dvalues)):
            fgrad[kv, fine_at] += grads[: 2 * BLOCK]
            mgrad[kv, mid_at] += grads[2 * BLOCK : 3 * BLOCK]
            rgrad[kv, far_at] += grads[3 * BLOCK :]

    def steps(step, carry):
        for inner in range(local):
            one_block(step, inner)
        return carry

    lax.fori_loop(0, blocks // local, steps, 0)

    for kv in range(2):
        pairs = mgrad[kv, 2 * HALF :] * 0.5
        fours = rgrad[kv, 6 * QUARTER :] * 0.25
        for lane in range(2):
            fgrad[kv, pl.ds(lane, (blocks + 1) * HALF, stride=2), :] += pairs
        for lane in range(4):
            fgrad[kv, pl.ds(lane, (blocks + 1) * QUARTER, stride=4), :] += fours
        shares = rgrad[kv, 4 * QUARTER : 6 * QUARTER] * 0.5
        for lane in range(2):
            mgrad[kv, pl.ds(lane, 2 * QUARTER, stride=2), :] += shares
        total[kv] = fgrad[kv, BLOCK:]
        back[kv, :BLOCK] = fgrad[kv, :BLOCK].astype(jnp.bfloat16)
        back[kv, BLOCK : BLOCK + 2 * HALF] = mgrad[kv, : 2 * HALF].astype(jnp.bfloat16)
        back[kv, BLOCK + 2 * HALF :] = rgrad[kv, : 4 * QUARTER].astype(jnp.bfloat16)


def attend(first_group, moved, fine, mid, far, halo):
    tokens = fine.shape[1]
    blocks = tokens // BLOCK
    f32 = jnp.float32
    flops = blocks * 6 * 2 * BLOCK * 4 * BLOCK * HD
    return pl.pallas_call(
        attend_body,
        out_shape=(
            jax.ShapeDtypeStruct(moved.shape, moved.dtype),
            jax.ShapeDtypeStruct((2, tokens, HD), f32),
            jax.ShapeDtypeStruct((2, BACK, HD), jnp.bfloat16),
        ),
        in_specs=[pl.BlockSpec(memory_space=pltpu.SMEM)] + whole(5),
        out_specs=tuple(whole(3)),
        scratch_shapes=[
            pltpu.VMEM((2, (blocks + 1) * BLOCK, HD), jnp.bfloat16),
            pltpu.VMEM((2, (blocks + 3) * HALF, HD), jnp.bfloat16),
            pltpu.VMEM((2, (blocks + 7) * QUARTER, HD), jnp.bfloat16),
            pltpu.VMEM((2, (blocks + 1) * BLOCK, HD), f32),
            pltpu.VMEM((2, (blocks + 3) * HALF, HD), f32),
            pltpu.VMEM((2, (blocks + 7) * QUARTER, HD), f32),
        ],
        compiler_params=params(),
        cost_estimate=cost(flops, 6 * 2**20),
    )(first_group, moved, fine, mid, far, halo)


def finish_body(total, back, out, scratch):
    sources, _, local, rows, _ = out.shape
    per_block = BLOCK // rows
    blocks = sources // per_block * local
    for kv in range(2):
        scratch[...] = total[kv]
        last = (blocks - 1) * BLOCK
        scratch[last:] += back[kv, :BLOCK].astype(jnp.float32)
        pairs = back[kv, BLOCK : BLOCK + 2 * HALF].astype(jnp.float32) * 0.5
        for lane in range(2):
            at = pl.ds((blocks - 3) * BLOCK + lane, 2 * HALF, stride=2)
            scratch[at, :] += pairs
        fours = back[kv, BLOCK + 2 * HALF :].astype(jnp.float32) * 0.25
        for lane in range(4):
            at = pl.ds((blocks - 7) * BLOCK + lane, 4 * QUARTER, stride=4)
            scratch[at, :] += fours
        for block in range(blocks):
            for part in range(per_block):
                start = block * BLOCK + part * rows
                source = block // local * per_block + part
                out[source, kv, block % local] = scratch[start : start + rows].astype(jnp.bfloat16)


def finish(total, back, shape):
    return pl.pallas_call(
        finish_body,
        out_shape=jax.ShapeDtypeStruct(shape, jnp.bfloat16),
        in_specs=whole(2),
        out_specs=whole(1)[0],
        scratch_shapes=[pltpu.VMEM(total.shape[1:], jnp.float32)],
        compiler_params=params(),
        cost_estimate=cost(0, total.size * 6),
    )(total, back)


def exchange(parts):
    return lax.all_to_all(parts, GROUP_AXES, split_axis=0, concat_axis=0, tiled=True)


def shifted(block, distance):
    devices = range(lax.axis_size("seq"))
    route = [(i - distance, i) for i in devices if i - distance in devices]
    return lax.ppermute(block, "seq", route)


def shards(queries, keys, values, cotangent):
    with jax.named_scope("keys_in"):
        moved_kv = exchange(spread(keys, values))
    with jax.named_scope("queries_in"):
        sent = spread(queries, cotangent)
        sent, moved_kv = lax.optimization_barrier((sent, moved_kv))
        moved_qc = exchange(sent)
    with jax.named_scope("halo"):
        fine, mid, far, msg = pool(moved_kv)
        halo = shifted(msg, 1)
    first_group = (lax.axis_index("seq") == 0).astype(jnp.int32).reshape(1)
    with jax.named_scope("attend"):
        out, total, back = attend(first_group, moved_qc, fine, mid, far, halo)
    with jax.named_scope("outputs_back"):
        moved_out = exchange(out)
    with jax.named_scope("halo_back"):
        received = shifted(back, -1)
        grads = finish(total, received, moved_kv.shape)
    with jax.named_scope("grads_back"):
        grads, moved_out = lax.optimization_barrier((grads, moved_out))
        moved_grads = exchange(grads)
    attended, grad_queries = join(moved_out)
    grad_keys, grad_values = join(moved_grads)
    return (attended, grad_queries, grad_keys, grad_values)


def solution(mesh):
    spec = P(("seq", "ctx"), "head", None)
    return jax.shard_map(
        shards, mesh=mesh, in_specs=(spec,) * 4, out_specs=(spec,) * 4, check_vma=False
    )
```

time: 389 us -> 113 us (0.29)
  the two profiles are of different devices: /device:TPU:102 before, /device:TPU:96 now
where the time goes in v1:
time: 113 us
  waiting for transfers between devices  59.2 us (52%)
  Pallas kernels  23.1 us (20%)
  starting transfers between devices  23.1 us (20%)
  local copies, waits for them, and re-layouts  6.55 us (6%)
    all_to_all x4, waiting for transfers between devices, exchange(): lax.all_to_all(parts, GROUP_AXES, split_axis=0, concat_axis=0, tiled=True)  45.8 us
    all_to_all x4, starting transfers between devices, exchange(): lax.all_to_all(parts, GROUP_AXES, split_axis=0, concat_axis=0, tiled=True)  19.2 us
    pallas_call x1, Pallas kernels, attend(): pl.pallas_call(attend_body, out_shape=(jax.ShapeDtypeStruct(moved.shape,...  15.4 us
    ppermute x2, waiting for transfers between devices, shifted(): return lax.ppermute(block, 'seq', route)  13.3 us
    unnamed x20, local copies, waits for them, and re-layouts  6.55 us
    ppermute x2, starting transfers between devices, shifted(): return lax.ppermute(block, 'seq', route)  3.83 us
    pallas_call x2, Pallas kernels, join(): pl.pallas_call(join_body, out_shape=(out, out), in_specs=whole(1), out_sp...  2.51 us
    pallas_call x2, Pallas kernels, spread(): pl.pallas_call(spread_body, out_shape=jax.ShapeDtypeStruct((heads, 2, blo...  2.33 us
  transfers between devices with their start and end apart: 6, of which 6 were waited for; matrix products, arithmetic and copies ran while one was open for 0% of the time, Pallas kernels for 5%

profile of v1, /device:TPU:96, one launch (start us, length us, event | category | flops | bytes accessed | tf_op | source)
XLA Modules:
  0.0 112.6 jit_solution(11778877977393795298)
XLA Ops:
  0.6 1.0 copy-done.2
  1.7 1.0 copy-done.3
  2.7 1.1 %keys_in.1 = bf16[16,2,2,64,128]{4,3,2,1,0:T(8,128)(2,1)} custom-call(bf16[2,64,2048]{2,1,0:T(8,128)(2,1)S(1)} %copy-done.2, bf16[2,64,2048]{2,1,0:T(8,128)(2,1)S(1)} %copy-done.3), custom_call_target="tpu_custom_call" | custom-call | bytes 2097152 | tf_op jit(solution)/shard_map/keys_in/pallas_call | solution.py:48
  3.9 7.0 %all-to-all-start = ((bf16[16,2,2,64,128]{4,3,2,1,0:T(8,128)(2,1)}), bf16[16,2,2,64,128]{4,3,2,1,0:T(8,128)(2,1)S(1)}, u32[]{:S(2)}, u32[]{:S(2)}) async-start(bf16[16,2,2,64,128]{4,3,2,1,0:T(8,128)(2,1)} %keys_in.1), calls=%async_computation | async-start | bytes 2097152 | tf_op jit(solution)/shard_map/keys_in/all_to_all | solution.py:311
  10.9 1.2 %queries_in.1 = bf16[16,2,2,64,128]{4,3,2,1,0:T(8,128)(2,1)} custom-call(bf16[2,64,2048]{2,1,0:T(8,128)(2,1)S(1)} %copy-done.4, bf16[2,64,2048]{2,1,0:T(8,128)(2,1)S(1)} %copy-done.5), custom_call_target="tpu_custom_call" | custom-call | bytes 2097152 | tf_op jit(solution)/shard_map/queries_in/pallas_call | solution.py:48
  12.1 16.5 %all-to-all-done.moved = bf16[16,2,2,64,128]{4,3,2,1,0:T(8,128)(2,1)S(1)} async-done(((bf16[16,2,2,64,128]{4,3,2,1,0:T(8,128)(2,1)}), bf16[16,2,2,64,128]{4,3,2,1,0:T(8,128)(2,1)S(1)}, u32[]{:S(2)}, u32[]{:S(2)}) %all-to-all-start) | async-done | bytes 1048608 | tf_op jit(solution)/shard_map/keys_in/all_to_all | solution.py:311
  28.6 3.7 %all-to-all-start.1 = ((bf16[16,2,2,64,128]{4,3,2,1,0:T(8,128)(2,1)}), bf16[16,2,2,64,128]{4,3,2,1,0:T(8,128)(2,1)S(1)}, u32[]{:S(2)}, u32[]{:S(2)}) async-start(bf16[16,2,2,64,128]{4,3,2,1,0:T(8,128)(2,1)} %queries_in.1), calls=%async_computation.1 | async-start | bytes 2097152 | tf_op jit(solution)/shard_map/queries_in/all_to_all | solution.py:311
  32.3 1.4 %halo.1 = (bf16[2,2048,128]{2,1,0:T(8,128)(2,1)S(1)}, bf16[2,1024,128]{2,1,0:T(8,128)(2,1)S(1)}, bf16[2,512,128]{2,1,0:T(8,128)(2,1)S(1)}, bf16[2,896,128]{2,1,0:T(8,128)(2,1)}) custom-call(bf16[16,2,2,64,128]{4,3,2,1,0:T(8,128)(2,1)S(1)} %all-to-all-done.moved), custom_call_target="tpu_custom_call" | custom-call | flops 201326592 | bytes 3145728 | tf_op jit(solution)/shard_map/halo/pallas_call | solution.py:117
  35.1 1.9 %collective-permute-start = (bf16[2,896,128]{2,1,0:T(8,128)(2,1)}, bf16[2,896,128]{2,1,0:T(8,128)(2,1)S(1)}, u32[]{:S(2)}, u32[]{:S(2)}) collective-permute-start(bf16[2,896,128]{2,1,0:T(8,128)(2,1)} %get-tuple-element.24), channel_id=1, source_target_pairs={{0,4},{4,8},{8,12},{12,16},{16,20},{20,24},{24,28},{28,32},{32,36}... | collective-permute-start | bytes 1376264 | tf_op jit(solution)/shard_map/halo/ppermute | solution.py:317
  37.0 8.1 %collective-permute-done.halo = bf16[2,896,128]{2,1,0:T(8,128)(2,1)S(1)} collective-permute-done((bf16[2,896,128]{2,1,0:T(8,128)(2,1)}, bf16[2,896,128]{2,1,0:T(8,128)(2,1)S(1)}, u32[]{:S(2)}, u32[]{:S(2)}) %collective-permute-start) | collective-permute-done | bytes 458784 | tf_op jit(solution)/shard_map/halo/ppermute | solution.py:317
  45.1 2.4 %all-to-all-done.1.moved = bf16[16,2,2,64,128]{4,3,2,1,0:T(8,128)(2,1)S(1)} async-done(((bf16[16,2,2,64,128]{4,3,2,1,0:T(8,128)(2,1)}), bf16[16,2,2,64,128]{4,3,2,1,0:T(8,128)(2,1)S(1)}, u32[]{:S(2)}, u32[]{:S(2)}) %all-to-all-start.1) | async-done | bytes 1048608 | tf_op jit(solution)/shard_map/queries_in/all_to_all | solution.py:311
  47.5 1.0 copy-done.7
  48.5 0.9 copy-done.9
  49.5 15.4 %attend.1 = (bf16[16,2,2,64,128]{4,3,2,1,0:T(8,128)(2,1)S(1)}, f32[2,2048,128]{2,1,0:T(8,128)}, bf16[2,768,128]{2,1,0:T(8,128)(2,1)S(1)}) custom-call(s32[1]{0:T(128)} %bitcast.first_group, bf16[16,2,2,64,128]{4,3,2,1,0:T(8,128)(2,1)S(1)} %all-to-all-done.1.moved, bf16[2,2048,128]{2,1,0:T(8,128)(2,1)S(1)} %get-tuple-element.21.fine, ...), custom_call_target="tpu_custom_call" | custom-call | flops 3221225472 | bytes 6291456 | tf_op jit(solution)/shard_map/attend/pallas_call | solution.py:253
  64.9 1.0 copy-done.1
  65.9 4.9 %all-to-all-start.2 = ((bf16[16,2,2,64,128]{4,3,2,1,0:T(8,128)(2,1)}), bf16[16,2,2,64,128]{4,3,2,1,0:T(8,128)(2,1)S(1)}, u32[]{:S(2)}, u32[]{:S(2)}) async-start(bf16[16,2,2,64,128]{4,3,2,1,0:T(8,128)(2,1)} %copy-done.1), calls=%async_computation.2 | async-start | bytes 2097152 | tf_op jit(solution)/shard_map/outputs_back/all_to_all | solution.py:311
  70.8 1.9 %collective-permute-start.1 = (bf16[2,768,128]{2,1,0:T(8,128)(2,1)S(1)}, bf16[2,768,128]{2,1,0:T(8,128)(2,1)S(1)}, u32[]{:S(2)}, u32[]{:S(2)}) collective-permute-start(bf16[2,768,128]{2,1,0:T(8,128)(2,1)S(1)} %get-tuple-element.26), channel_id=1, source_target_pairs={{4,0},{8,4},{12,8},{16,12},{20,16},{24,20},{28,24},{32,28},{36,32}... | collective-permute-start | bytes 1179656 | tf_op jit(solution)/shard_map/halo_back/ppermute | solution.py:317
  72.7 5.3 %collective-permute-done.1.back = bf16[2,768,128]{2,1,0:T(8,128)(2,1)S(1)} collective-permute-done((bf16[2,768,128]{2,1,0:T(8,128)(2,1)S(1)}, bf16[2,768,128]{2,1,0:T(8,128)(2,1)S(1)}, u32[]{:S(2)}, u32[]{:S(2)}) %collective-permute-start.1) | collective-permute-done | bytes 393248 | tf_op jit(solution)/shard_map/halo_back/ppermute | solution.py:317
  78.0 1.4 %halo_back.1 = bf16[16,2,2,64,128]{4,3,2,1,0:T(8,128)(2,1)} custom-call(f32[2,2048,128]{2,1,0:T(8,128)S(1)} %copy-done, bf16[2,768,128]{2,1,0:T(8,128)(2,1)S(1)} %collective-permute-done.1.back), custom_call_target="tpu_custom_call" | custom-call | bytes 3145728 | tf_op jit(solution)/shard_map/halo_back/pallas_call | solution.py:299
  79.5 10.6 %all-to-all-done.2.moved = bf16[16,2,2,64,128]{4,3,2,1,0:T(8,128)(2,1)S(1)} async-done(((bf16[16,2,2,64,128]{4,3,2,1,0:T(8,128)(2,1)}), bf16[16,2,2,64,128]{4,3,2,1,0:T(8,128)(2,1)S(1)}, u32[]{:S(2)}, u32[]{:S(2)}) %all-to-all-start.2) | async-done | bytes 1048608 | tf_op jit(solution)/shard_map/outputs_back/all_to_all | solution.py:311
  90.1 3.7 %all-to-all-start.3 = ((bf16[16,2,2,64,128]{4,3,2,1,0:T(8,128)(2,1)}), bf16[16,2,2,64,128]{4,3,2,1,0:T(8,128)(2,1)S(1)}, u32[]{:S(2)}, u32[]{:S(2)}) async-start(bf16[16,2,2,64,128]{4,3,2,1,0:T(8,128)(2,1)} %halo_back.1), calls=%async_computation.3 | async-start | bytes 2097152 | tf_op jit(solution)/shard_map/grads_back/all_to_all | solution.py:311
  93.7 1.3 %shard_map.75 = (bf16[2,64,2048]{2,1,0:T(8,128)(2,1)}, bf16[2,64,2048]{2,1,0:T(8,128)(2,1)}) custom-call(bf16[16,2,2,64,128]{4,3,2,1,0:T(8,128)(2,1)S(1)} %all-to-all-done.2.moved), custom_call_target="tpu_custom_call" | custom-call | bytes 2097152 | tf_op jit(solution)/shard_map/pallas_call | solution.py:67
  95.0 16.3 %all-to-all-done.3.moved = bf16[16,2,2,64,128]{4,3,2,1,0:T(8,128)(2,1)S(1)} async-done(((bf16[16,2,2,64,128]{4,3,2,1,0:T(8,128)(2,1)}), bf16[16,2,2,64,128]{4,3,2,1,0:T(8,128)(2,1)S(1)}, u32[]{:S(2)}, u32[]{:S(2)}) %all-to-all-start.3) | async-done | bytes 1048608 | tf_op jit(solution)/shard_map/grads_back/all_to_all | solution.py:311
  111.3 1.3 %shard_map.76 = (bf16[2,64,2048]{2,1,0:T(8,128)(2,1)}, bf16[2,64,2048]{2,1,0:T(8,128)(2,1)}) custom-call(bf16[16,2,2,64,128]{4,3,2,1,0:T(8,128)(2,1)S(1)} %all-to-all-done.3.moved), custom_call_target="tpu_custom_call" | custom-call | bytes 2097152 | tf_op jit(solution)/shard_map/pallas_call | solution.py:67
  (15 shorter events, 1.5 us)
Async XLA Ops:
  0.6 1.0 copy-start.2
  1.7 1.0 copy-start.3
  2.7 8.2 %copy-start.4 = (bf16[2,64,2048]{2,1,0:T(8,128)(2,1)S(1)}, bf16[2,64,2048]{2,1,0:T(8,128)(2,1)}, u32[]{:S(2)}) copy-start(bf16[2,64,2048]{2,1,0:T(8,128)(2,1)} %first.2) | copy-start | bytes 1572868
  2.7 8.2 %copy-start.5 = (bf16[2,64,2048]{2,1,0:T(8,128)(2,1)S(1)}, bf16[2,64,2048]{2,1,0:T(8,128)(2,1)}, u32[]{:S(2)}) copy-start(bf16[2,64,2048]{2,1,0:T(8,128)(2,1)} %second.2) | copy-start | bytes 1572868
  3.9 24.7 %all-to-all-start = ((bf16[16,2,2,64,128]{4,3,2,1,0:T(8,128)(2,1)}), bf16[16,2,2,64,128]{4,3,2,1,0:T(8,128)(2,1)S(1)}, u32[]{:S(2)}, u32[]{:S(2)}) async-start(bf16[16,2,2,64,128]{4,3,2,1,0:T(8,128)(2,1)} %keys_in.1), calls=%async_computation | async-start | bytes 2097152 | tf_op jit(solution)/shard_map/keys_in/all_to_all | solution.py:311
  28.6 18.9 %all-to-all-start.1 = ((bf16[16,2,2,64,128]{4,3,2,1,0:T(8,128)(2,1)}), bf16[16,2,2,64,128]{4,3,2,1,0:T(8,128)(2,1)S(1)}, u32[]{:S(2)}, u32[]{:S(2)}) async-start(bf16[16,2,2,64,128]{4,3,2,1,0:T(8,128)(2,1)} %queries_in.1), calls=%async_computation.1 | async-start | bytes 2097152 | tf_op jit(solution)/shard_map/queries_in/all_to_all | solution.py:311
  33.6 0.8 copy-start.6
  34.4 0.7 copy-start.8
  35.1 10.0 %collective-permute-start = (bf16[2,896,128]{2,1,0:T(8,128)(2,1)}, bf16[2,896,128]{2,1,0:T(8,128)(2,1)S(1)}, u32[]{:S(2)}, u32[]{:S(2)}) collective-permute-start(bf16[2,896,128]{2,1,0:T(8,128)(2,1)} %get-tuple-element.24), channel_id=1, source_target_pairs={{0,4},{4,8},{8,12},{12,16},{16,20},{20,24},{24,28},{28,32},{32,36}... | collective-permute-start | bytes 1376264 | tf_op jit(solution)/shard_map/halo/ppermute | solution.py:317
  47.5 1.0 copy-start.7
  48.5 0.9 copy-start.9
  64.9 1.0 copy-start.1
  65.9 12.1 %copy-start = (f32[2,2048,128]{2,1,0:T(8,128)S(1)}, f32[2,2048,128]{2,1,0:T(8,128)}, u32[]{:S(2)}) copy-start(f32[2,2048,128]{2,1,0:T(8,128)} %get-tuple-element.25.total) | copy-start | bytes 6291460
  65.9 24.2 %all-to-all-start.2 = ((bf16[16,2,2,64,128]{4,3,2,1,0:T(8,128)(2,1)}), bf16[16,2,2,64,128]{4,3,2,1,0:T(8,128)(2,1)S(1)}, u32[]{:S(2)}, u32[]{:S(2)}) async-start(bf16[16,2,2,64,128]{4,3,2,1,0:T(8,128)(2,1)} %copy-done.1), calls=%async_computation.2 | async-start | bytes 2097152 | tf_op jit(solution)/shard_map/outputs_back/all_to_all | solution.py:311
  70.8 7.2 %collective-permute-start.1 = (bf16[2,768,128]{2,1,0:T(8,128)(2,1)S(1)}, bf16[2,768,128]{2,1,0:T(8,128)(2,1)S(1)}, u32[]{:S(2)}, u32[]{:S(2)}) collective-permute-start(bf16[2,768,128]{2,1,0:T(8,128)(2,1)S(1)} %get-tuple-element.26), channel_id=1, source_target_pairs={{4,0},{8,4},{12,8},{16,12},{20,16},{24,20},{28,24},{32,28},{36,32}... | collective-permute-start | bytes 1179656 | tf_op jit(solution)/shard_map/halo_back/ppermute | solution.py:317
  90.1 21.3 %all-to-all-start.3 = ((bf16[16,2,2,64,128]{4,3,2,1,0:T(8,128)(2,1)}), bf16[16,2,2,64,128]{4,3,2,1,0:T(8,128)(2,1)S(1)}, u32[]{:S(2)}, u32[]{:S(2)}) async-start(bf16[16,2,2,64,128]{4,3,2,1,0:T(8,128)(2,1)} %halo_back.1), calls=%async_computation.3 | async-start | bytes 2097152 | tf_op jit(solution)/shard_map/grads_back/all_to_all | solution.py:311

commit v2 on v1

v2 whole, which is shorter than its diff:
```python
import functools
import math

import jax
import jax.numpy as jnp
from jax import lax
from jax.experimental import pallas as pl
from jax.experimental.pallas import tpu as pltpu
from jax.sharding import PartitionSpec as P

HD = 128
BLOCK = 256
HALF = BLOCK // 2
QUARTER = BLOCK // 4
SCALE = 1.0 / math.sqrt(HD)
LOG2E = 1.0 / math.log(2.0)
NEG = -1e30
HALO_FINE = BLOCK
HALO_MID = 2 * HALF
HALO_FAR = 6 * QUARTER
HALO = HALO_FINE + HALO_MID + HALO_FAR
BACK = BLOCK + 2 * HALF + 4 * QUARTER
GROUP_AXES = ("ctx", "head")


def whole(count):
    return [pl.BlockSpec(memory_space=pltpu.VMEM)] * count


def params(mebibytes):
    return pltpu.CompilerParams(vmem_limit_bytes=mebibytes * 2**20)


def cost(flops, nbytes):
    return pl.CostEstimate(flops=flops, bytes_accessed=nbytes, transcendentals=0)


def spread_body(*refs):
    count = (len(refs) - 2) // 2
    sources, out, held, sems = refs[:count], refs[count], refs[count + 1 : -1], refs[-1]
    blocks = out.shape[2]
    copies = {}
    for which in range(count):
        for block in range(blocks):
            copies[which, block] = pltpu.make_async_copy(
                sources[which].at[block], held[which].at[block], sems.at[which, block]
            )
            copies[which, block].start()
    for which in range(count):
        for block in range(blocks):
            copies[which, block].wait()
            for head in range(out.shape[0]):
                out[head, which, block] = held[which][block, :, head * HD : (head + 1) * HD]


def spread(*arrays):
    blocks, rows, features = arrays[0].shape
    heads = features // HD
    count = len(arrays)
    return pl.pallas_call(
        spread_body,
        out_shape=jax.ShapeDtypeStruct((heads, count, blocks, rows, HD), arrays[0].dtype),
        in_specs=[pl.BlockSpec(memory_space=pltpu.HBM)] * count,
        out_specs=whole(1)[0],
        scratch_shapes=[pltpu.VMEM((blocks, rows, features), arrays[0].dtype)] * count
        + [pltpu.SemaphoreType.DMA((count, blocks))],
        compiler_params=params(58),
        cost_estimate=cost(0, 4 * count * arrays[0].size),
    )(*arrays)


def join_body(moved, *outs):
    for which, out in enumerate(outs):
        for head in range(moved.shape[0]):
            out[:, :, head * HD : (head + 1) * HD] = moved[head, which]


def join(moved):
    heads, count, blocks, rows, _ = moved.shape
    out = jax.ShapeDtypeStruct((blocks, rows, heads * HD), moved.dtype)
    return pl.pallas_call(
        join_body,
        out_shape=(out,) * count,
        in_specs=whole(1),
        out_specs=tuple(whole(count)),
        compiler_params=params(8),
        cost_estimate=cost(0, 4 * moved.size),
    )(moved)


def pool_matrix():
    row = lax.broadcasted_iota(jnp.int32, (HALF + QUARTER, BLOCK), 0)
    col = lax.broadcasted_iota(jnp.int32, (HALF + QUARTER, BLOCK), 1)
    pair = (row < HALF) & ((col >> 1) == row)
    four = (row >= HALF) & ((col >> 2) == row - HALF)
    both = jnp.where(pair, 0.5, 0.0) + jnp.where(four, 0.25, 0.0)
    return both.astype(jnp.bfloat16)


def sizes(moved):
    sources, _, local, rows, _ = moved.shape
    per_block = BLOCK // rows
    return sources // per_block * local, local, per_block, rows


def tokens_of(moved, which, step, inner):
    per_block = BLOCK // moved.shape[3]
    return jnp.concatenate(
        [moved[step * per_block + part, which, inner] for part in range(per_block)], axis=0
    )


def places(block):
    return (
        pl.ds(pl.multiple_of(block * BLOCK, BLOCK), 2 * BLOCK),
        pl.ds(pl.multiple_of(block * HALF, HALF), 2 * HALF),
        pl.ds(pl.multiple_of(block * QUARTER, QUARTER), 4 * QUARTER),
    )


def window(extended, kv, block):
    return jnp.concatenate([ref[kv, at] for ref, at in zip(extended, places(block))], axis=0)


def store_rows(out, which, step, inner, value):
    rows = out.shape[3]
    per_block = BLOCK // rows
    for part in range(per_block):
        out[step * per_block + part, which, inner] = value[part * rows : (part + 1) * rows]


def each_block(moved, one_block):
    blocks, local, _, _ = sizes(moved)

    def steps(step, carry):
        for inner in range(local):
            one_block(step, inner, step * local + inner)
        return carry

    lax.fori_loop(0, blocks // local, steps, 0)


def pooled_rows(matrix, tokens):
    return jnp.dot(matrix, tokens, preferred_element_type=jnp.float32).astype(jnp.bfloat16)


def message_body(moved, msg):
    blocks, local, _, _ = sizes(moved)
    matrix = pool_matrix()
    for kv in range(2):
        for from_end in range(1, 8):
            block = blocks - from_end
            tokens = tokens_of(moved, kv, block // local, block % local)
            if from_end == 1:
                msg[kv, :HALO_FINE] = tokens
                continue
            pooled = pooled_rows(matrix, tokens)
            if from_end <= 3:
                start = HALO_FINE + (3 - from_end) * HALF
                msg[kv, start : start + HALF] = pooled[:HALF]
            start = HALO_FINE + HALO_MID + (7 - from_end) * QUARTER
            msg[kv, start : start + QUARTER] = pooled[HALF:]


def message(moved):
    return pl.pallas_call(
        message_body,
        out_shape=jax.ShapeDtypeStruct((2, HALO, HD), jnp.bfloat16),
        in_specs=whole(1),
        out_specs=whole(1)[0],
        compiler_params=params(8),
        cost_estimate=cost(4 * 6 * 192 * BLOCK * HD, moved.size * 2),
    )(moved)


def dot_nt(a, b):
    return lax.dot_general(a, b, (((1,), (1,)), ((), ())), preferred_element_type=jnp.float32)


def dot_tn(a, b):
    return lax.dot_general(a, b, (((0,), (0,)), ((), ())), preferred_element_type=jnp.float32)


def dot_nn(a, b):
    return jnp.dot(a, b, preferred_element_type=jnp.float32)


def extend(moved, halo, fext, mext, rext):
    blocks, local, _, _ = sizes(moved)
    matrix = pool_matrix()
    for kv in range(2):
        mext[kv, : 2 * HALF] = halo[kv, HALO_FINE : HALO_FINE + HALO_MID]
        rext[kv, : 6 * QUARTER] = halo[kv, HALO_FINE + HALO_MID :]
        for block in range(-1, blocks):
            if block < 0:
                tokens = halo[kv, :HALO_FINE]
            else:
                tokens = tokens_of(moved, kv, block // local, block % local)
            pooled = pooled_rows(matrix, tokens)
            fext[kv, (block + 1) * BLOCK : (block + 2) * BLOCK] = tokens
            mext[kv, (block + 3) * HALF : (block + 4) * HALF] = pooled[:HALF]
            rext[kv, (block + 7) * QUARTER : (block + 8) * QUARTER] = pooled[HALF:]


def attend_body(
    first_group,
    moved,
    moved_kv,
    halo,
    out,
    total,
    back,
    fext,
    mext,
    rext,
    fgrad,
    mgrad,
    rgrad,
):
    blocks, local, per_block, rows = sizes(moved)
    extend(moved_kv, halo, fext, mext, rext)
    fgrad[...] = jnp.zeros_like(fgrad)
    mgrad[...] = jnp.zeros_like(mgrad)
    rgrad[...] = jnp.zeros_like(rgrad)
    is_first = first_group[0]
    extended = (fext, mext, rext)

    def one_block(step, inner, block):
        queries = tokens_of(moved, 0, step, inner)
        cotangent = tokens_of(moved, 1, step, inner)
        keyset = window(extended, 0, block)
        valset = window(extended, 1, block)
        scores = dot_nt(keyset, queries)
        row = lax.broadcasted_iota(jnp.int32, (BLOCK, BLOCK), 0)
        col = lax.broadcasted_iota(jnp.int32, (BLOCK, BLOCK), 1)
        absent = is_first * jnp.maximum(1 - block, 0) * BLOCK
        absent_mid = is_first * jnp.maximum(3 - block, 0) * HALF
        absent_far = is_first * jnp.maximum(7 - block, 0) * QUARTER
        scores = jnp.concatenate(
            [
                jnp.where(row < absent, NEG, scores[:BLOCK]),
                jnp.where(row <= col, scores[BLOCK : 2 * BLOCK], NEG),
                jnp.where(row < absent_mid, NEG, scores[2 * BLOCK : 3 * BLOCK]),
                jnp.where(row < absent_far, NEG, scores[3 * BLOCK :]),
            ],
            axis=0,
        )
        top = jnp.max(scores, axis=0, keepdims=True)
        powers = jnp.exp2((scores - top) * (SCALE * LOG2E))
        norm = 1.0 / jnp.sum(powers, axis=0, keepdims=True)
        normed = powers * norm
        weights = normed.astype(jnp.bfloat16)
        attended = dot_tn(valset, weights)
        turned = jnp.transpose(cotangent.astype(jnp.float32))
        delta = jnp.sum(attended * turned, axis=0, keepdims=True)
        dweights = dot_nt(valset, cotangent)
        dscores = (normed * (dweights - delta)).astype(jnp.bfloat16)
        dqueries = dot_tn(keyset, dscores) * SCALE
        dkeys = dot_nn(dscores, queries) * SCALE
        dvalues = dot_nn(weights, cotangent)
        store_rows(out, 0, step, inner, jnp.transpose(attended).astype(jnp.bfloat16))
        store_rows(out, 1, step, inner, jnp.transpose(dqueries).astype(jnp.bfloat16))
        fine_at, mid_at, far_at = places(block)
        for kv, grads in enumerate((dkeys, dvalues)):
            fgrad[kv, fine_at] += grads[: 2 * BLOCK]
            mgrad[kv, mid_at] += grads[2 * BLOCK : 3 * BLOCK]
            rgrad[kv, far_at] += grads[3 * BLOCK :]

    each_block(moved, one_block)
    for kv in range(2):
        pairs = mgrad[kv, 2 * HALF :] * 0.5
        fours = rgrad[kv, 6 * QUARTER :] * 0.25
        for lane in range(2):
            fgrad[kv, pl.ds(lane, (blocks + 1) * HALF, stride=2), :] += pairs
        for lane in range(4):
            fgrad[kv, pl.ds(lane, (blocks + 1) * QUARTER, stride=4), :] += fours
        shares = rgrad[kv, 4 * QUARTER : 6 * QUARTER] * 0.5
        for lane in range(2):
            mgrad[kv, pl.ds(lane, 2 * QUARTER, stride=2), :] += shares
        total[kv] = fgrad[kv, BLOCK:]
        back[kv, :BLOCK] = fgrad[kv, :BLOCK].astype(jnp.bfloat16)
        back[kv, BLOCK : BLOCK + 2 * HALF] = mgrad[kv, : 2 * HALF].astype(jnp.bfloat16)
        back[kv, BLOCK + 2 * HALF :] = rgrad[kv, : 4 * QUARTER].astype(jnp.bfloat16)


def attend(first_group, moved, moved_kv, halo):
    blocks, local, per_block, rows = sizes(moved)
    f32 = jnp.float32
    return pl.pallas_call(
        attend_body,
        out_shape=(
            jax.ShapeDtypeStruct((moved.shape[0], 4) + moved.shape[2:], moved.dtype),
            jax.ShapeDtypeStruct((2, blocks * BLOCK, HD), f32),
            jax.ShapeDtypeStruct((2, BACK, HD), jnp.bfloat16),
        ),
        in_specs=[pl.BlockSpec(memory_space=pltpu.SMEM)] + whole(3),
        out_specs=tuple(whole(3)),
        scratch_shapes=[
            pltpu.VMEM((2, (blocks + 1) * BLOCK, HD), jnp.bfloat16),
            pltpu.VMEM((2, (blocks + 3) * HALF, HD), jnp.bfloat16),
            pltpu.VMEM((2, (blocks + 7) * QUARTER, HD), jnp.bfloat16),
            pltpu.VMEM((2, (blocks + 1) * BLOCK, HD), f32),
            pltpu.VMEM((2, (blocks + 3) * HALF, HD), f32),
            pltpu.VMEM((2, (blocks + 7) * QUARTER, HD), f32),
        ],
        compiler_params=params(24),
        cost_estimate=cost(blocks * 12 * BLOCK * 4 * BLOCK * HD, 8 * 2**20),
    )(first_group, moved, moved_kv, halo)


def finish_body(total, back, given, out, scratch):
    sources, _, local, rows, _ = out.shape
    per_block = BLOCK // rows
    blocks = sources // per_block * local
    for kv in range(2):
        scratch[...] = total[kv]
        last = (blocks - 1) * BLOCK
        scratch[last:] += back[kv, :BLOCK].astype(jnp.float32)
        pairs = back[kv, BLOCK : BLOCK + 2 * HALF].astype(jnp.float32) * 0.5
        for lane in range(2):
            at = pl.ds((blocks - 3) * BLOCK + lane, 2 * HALF, stride=2)
            scratch[at, :] += pairs
        fours = back[kv, BLOCK + 2 * HALF :].astype(jnp.float32) * 0.25
        for lane in range(4):
            at = pl.ds((blocks - 7) * BLOCK + lane, 4 * QUARTER, stride=4)
            scratch[at, :] += fours
        for source in range(sources):
            for inner in range(local):
                start = (source // per_block * local + inner) * BLOCK + source % per_block * rows
                piece = scratch[start : start + rows].astype(jnp.bfloat16)
                out[source, 2 + kv, inner] = piece


def finish(total, back, out):
    return pl.pallas_call(
        finish_body,
        out_shape=jax.ShapeDtypeStruct(out.shape, out.dtype),
        in_specs=whole(2) + [pl.BlockSpec(memory_space=pltpu.VMEM)],
        out_specs=whole(1)[0],
        scratch_shapes=[pltpu.VMEM(total.shape[1:], jnp.float32)],
        input_output_aliases={2: 0},
        compiler_params=params(12),
        cost_estimate=cost(0, total.size * 6),
    )(total, back, out)


def exchange(parts):
    return lax.all_to_all(parts, GROUP_AXES, split_axis=0, concat_axis=0, tiled=True)


def shifted(block, distance):
    devices = range(lax.axis_size("seq"))
    route = [(i - distance, i) for i in devices if i - distance in devices]
    return lax.ppermute(block, "seq", route)


def shards(queries, keys, values, cotangent):
    first_group = (lax.axis_index("seq") == 0).astype(jnp.int32).reshape(1)
    with jax.named_scope("keys_in"):
        moved_kv = exchange(spread(keys, values))
    with jax.named_scope("queries_in"):
        sent, moved_kv = lax.optimization_barrier((spread(queries, cotangent), moved_kv))
        moved = exchange(sent)
    with jax.named_scope("halo"):
        halo = shifted(message(moved_kv), 1)
    with jax.named_scope("attend"):
        out, total, back = attend(first_group, moved, moved_kv, halo)
    with jax.named_scope("halo_back"):
        out = finish(total, shifted(back, -1), out)
    with jax.named_scope("outputs"):
        return join(exchange(out))


def solution(mesh):
    spec = P(("seq", "ctx"), "head", None)
    return jax.shard_map(
        shards, mesh=mesh, in_specs=(spec,) * 4, out_specs=(spec,) * 4, check_vma=False
    )
```

time: 113 us -> 104 us (0.920)
  the two profiles are of different devices: /device:TPU:96 before, /device:TPU:33 now
where the time goes in v2:
time: 104 us
  blocking collectives  30.8 us (30%)
  waiting for transfers between devices  27.8 us (27%)
  starting transfers between devices  22.6 us (22%)
  Pallas kernels  21.8 us (21%)
    all_to_all x1, blocking collectives, exchange(): lax.all_to_all(parts, GROUP_AXES, split_axis=0, concat_axis=0, tiled=True)  30.8 us
    all_to_all x2, waiting for transfers between devices, exchange(): lax.all_to_all(parts, GROUP_AXES, split_axis=0, concat_axis=0, tiled=True)  15.5 us
    pallas_call x1, Pallas kernels, attend(): pl.pallas_call(attend_body, out_shape=(jax.ShapeDtypeStruct((moved.shape[...  14.5 us
    ppermute x2, waiting for transfers between devices, shifted(): return lax.ppermute(block, 'seq', route)  12.4 us
    ppermute x2, starting transfers between devices, shifted(): return lax.ppermute(block, 'seq', route)  11.9 us
    all_to_all x2, starting transfers between devices, exchange(): lax.all_to_all(parts, GROUP_AXES, split_axis=0, concat_axis=0, tiled=True)  10.7 us
    pallas_call x2, Pallas kernels, spread(): pl.pallas_call(spread_body, out_shape=jax.ShapeDtypeStruct((heads, count,...  4.55 us
  transfers between devices with their start and end apart: 4, of which 4 were waited for; matrix products, arithmetic and copies ran while one was open for 0% of the time, Pallas kernels for 3%

profile of v2, /device:TPU:33, one launch (start us, length us, event | category | flops | bytes accessed | tf_op | source)
XLA Modules:
  0.0 103.7 jit_solution(7430640146663890219)
XLA Ops:
  0.6 2.3 %keys_in.1 = bf16[16,2,2,64,128]{4,3,2,1,0:T(8,128)(2,1)} custom-call(bf16[2,64,2048]{2,1,0:T(8,128)(2,1)} %refs_0_.3, bf16[2,64,2048]{2,1,0:T(8,128)(2,1)} %refs_1_.3), custom_call_target="tpu_custom_call" | custom-call | bytes 2097152 | tf_op jit(solution)/shard_map/keys_in/pallas_call | solution.py:60
  2.9 6.8 %all-to-all-start = ((bf16[16,2,2,64,128]{4,3,2,1,0:T(8,128)(2,1)}), bf16[16,2,2,64,128]{4,3,2,1,0:T(8,128)(2,1)S(1)}, u32[]{:S(2)}, u32[]{:S(2)}) async-start(bf16[16,2,2,64,128]{4,3,2,1,0:T(8,128)(2,1)} %keys_in.1), calls=%async_computation | async-start | bytes 2097152 | tf_op jit(solution)/shard_map/keys_in/all_to_all | solution.py:348
  9.7 2.2 %queries_in.1 = bf16[16,2,2,64,128]{4,3,2,1,0:T(8,128)(2,1)} custom-call(bf16[2,64,2048]{2,1,0:T(8,128)(2,1)} %refs_0_.2, bf16[2,64,2048]{2,1,0:T(8,128)(2,1)} %refs_1_.2), custom_call_target="tpu_custom_call" | custom-call | bytes 2097152 | tf_op jit(solution)/shard_map/queries_in/pallas_call | solution.py:60
  12.0 13.3 %all-to-all-done.moved.moved_kv = bf16[16,2,2,64,128]{4,3,2,1,0:T(8,128)(2,1)S(1)} async-done(((bf16[16,2,2,64,128]{4,3,2,1,0:T(8,128)(2,1)}), bf16[16,2,2,64,128]{4,3,2,1,0:T(8,128)(2,1)S(1)}, u32[]{:S(2)}, u32[]{:S(2)}) %all-to-all-start) | async-done | bytes 1048608 | tf_op jit(solution)/shard_map/keys_in/all_to_all | solution.py:348
  25.2 4.0 %all-to-all-start.1 = ((bf16[16,2,2,64,128]{4,3,2,1,0:T(8,128)(2,1)}), bf16[16,2,2,64,128]{4,3,2,1,0:T(8,128)(2,1)S(1)}, u32[]{:S(2)}, u32[]{:S(2)}) async-start(bf16[16,2,2,64,128]{4,3,2,1,0:T(8,128)(2,1)} %queries_in.1), calls=%async_computation.1 | async-start | bytes 2097152 | tf_op jit(solution)/shard_map/queries_in/all_to_all | solution.py:348
  29.2 0.5 halo.1
  29.7 6.3 %collective-permute-start = (bf16[2,896,128]{2,1,0:T(8,128)(2,1)S(1)}, bf16[2,896,128]{2,1,0:T(8,128)(2,1)S(1)}, u32[]{:S(2)}, u32[]{:S(2)}) collective-permute-start(bf16[2,896,128]{2,1,0:T(8,128)(2,1)S(1)} %halo.1), channel_id=1, source_target_pairs={{0,4},{4,8},{8,12},{12,16},{16,20},{20,24},{24,28},{28,32},{32,36}... | collective-permute-start | bytes 1376264 | tf_op jit(solution)/shard_map/halo/ppermute | solution.py:354
  35.9 5.4 %collective-permute-done.halo = bf16[2,896,128]{2,1,0:T(8,128)(2,1)S(1)} collective-permute-done((bf16[2,896,128]{2,1,0:T(8,128)(2,1)S(1)}, bf16[2,896,128]{2,1,0:T(8,128)(2,1)S(1)}, u32[]{:S(2)}, u32[]{:S(2)}) %collective-permute-start) | collective-permute-done | bytes 458784 | tf_op jit(solution)/shard_map/halo/ppermute | solution.py:354
  41.3 2.2 %all-to-all-done.1.moved = bf16[16,2,2,64,128]{4,3,2,1,0:T(8,128)(2,1)S(1)} async-done(((bf16[16,2,2,64,128]{4,3,2,1,0:T(8,128)(2,1)}), bf16[16,2,2,64,128]{4,3,2,1,0:T(8,128)(2,1)S(1)}, u32[]{:S(2)}, u32[]{:S(2)}) %all-to-all-start.1) | async-done | bytes 1048608 | tf_op jit(solution)/shard_map/queries_in/all_to_all | solution.py:348
  43.5 14.5 %attend.1 = (bf16[16,4,2,64,128]{4,3,2,1,0:T(8,128)(2,1)S(1)}, f32[2,2048,128]{2,1,0:T(8,128)S(1)}, bf16[2,768,128]{2,1,0:T(8,128)(2,1)S(1)}) custom-call(s32[1]{0:T(128)} %bitcast.first_group, bf16[16,2,2,64,128]{4,3,2,1,0:T(8,128)(2,1)S(1)} %all-to-all-done.1.moved, bf16[16,2,2,64,128]{4,3,2,1,0:T(8,128)(2,1)S(1)} %all-to-all-done.moved.moved_kv, ...), custom_call_target="tpu_custom_call" | custom-call | flops 3221225472 | bytes 8388608 | tf_op jit(solution)/shard_map/attend/pallas_call | solution.py:289
  58.1 5.6 %collective-permute-start.1 = (bf16[2,768,128]{2,1,0:T(8,128)(2,1)S(1)}, bf16[2,768,128]{2,1,0:T(8,128)(2,1)S(1)}, u32[]{:S(2)}, u32[]{:S(2)}) collective-permute-start(bf16[2,768,128]{2,1,0:T(8,128)(2,1)S(1)} %get-tuple-element.12), channel_id=1, source_target_pairs={{4,0},{8,4},{12,8},{16,12},{20,16},{24,20},{28,24},{32,28},{36,32}... | collective-permute-start | bytes 1179656 | tf_op jit(solution)/shard_map/halo_back/ppermute | solution.py:354
  63.7 7.0 %collective-permute-done.1.back = bf16[2,768,128]{2,1,0:T(8,128)(2,1)S(1)} collective-permute-done((bf16[2,768,128]{2,1,0:T(8,128)(2,1)S(1)}, bf16[2,768,128]{2,1,0:T(8,128)(2,1)S(1)}, u32[]{:S(2)}, u32[]{:S(2)}) %collective-permute-start.1) | collective-permute-done | bytes 393248 | tf_op jit(solution)/shard_map/halo_back/ppermute | solution.py:354
  70.7 0.4 halo_back.1
  71.1 30.8 %all_to_all.15.moved = bf16[16,4,2,64,128]{4,3,2,1,0:T(8,128)(2,1)S(1)} all-to-all(bf16[16,4,2,64,128]{4,3,2,1,0:T(8,128)(2,1)S(1)} %halo_back.1), channel_id=1, replica_groups=mesh['head'=4,'seq'=16,'ctx'=4] {'ctx','head'}, dimensions={0} | all-to-all | bytes 4194304 | tf_op jit(solution)/shard_map/outputs/all_to_all | solution.py:348
  101.9 1.9 %outputs.1 = (bf16[2,64,2048]{2,1,0:T(8,128)(2,1)}, bf16[2,64,2048]{2,1,0:T(8,128)(2,1)}, bf16[2,64,2048]{2,1,0:T(8,128)(2,1)}, bf16[2,64,2048]{2,1,0:T(8,128)(2,1)}) custom-call(bf16[16,4,2,64,128]{4,3,2,1,0:T(8,128)(2,1)S(1)} %all_to_all.15.moved), custom_call_target="tpu_custom_call" | custom-call | bytes 4194304 | tf_op jit(solution)/shard_map/outputs/pallas_call | solution.py:81
Async XLA Ops:
  2.9 22.3 %all-to-all-start = ((bf16[16,2,2,64,128]{4,3,2,1,0:T(8,128)(2,1)}), bf16[16,2,2,64,128]{4,3,2,1,0:T(8,128)(2,1)S(1)}, u32[]{:S(2)}, u32[]{:S(2)}) async-start(bf16[16,2,2,64,128]{4,3,2,1,0:T(8,128)(2,1)} %keys_in.1), calls=%async_computation | async-start | bytes 2097152 | tf_op jit(solution)/shard_map/keys_in/all_to_all | solution.py:348
  25.2 18.3 %all-to-all-start.1 = ((bf16[16,2,2,64,128]{4,3,2,1,0:T(8,128)(2,1)}), bf16[16,2,2,64,128]{4,3,2,1,0:T(8,128)(2,1)S(1)}, u32[]{:S(2)}, u32[]{:S(2)}) async-start(bf16[16,2,2,64,128]{4,3,2,1,0:T(8,128)(2,1)} %queries_in.1), calls=%async_computation.1 | async-start | bytes 2097152 | tf_op jit(solution)/shard_map/queries_in/all_to_all | solution.py:348
  29.7 11.7 %collective-permute-start = (bf16[2,896,128]{2,1,0:T(8,128)(2,1)S(1)}, bf16[2,896,128]{2,1,0:T(8,128)(2,1)S(1)}, u32[]{:S(2)}, u32[]{:S(2)}) collective-permute-start(bf16[2,896,128]{2,1,0:T(8,128)(2,1)S(1)} %halo.1), channel_id=1, source_target_pairs={{0,4},{4,8},{8,12},{12,16},{16,20},{20,24},{24,28},{28,32},{32,36}... | collective-permute-start | bytes 1376264 | tf_op jit(solution)/shard_map/halo/ppermute | solution.py:354
  58.1 12.6 %collective-permute-start.1 = (bf16[2,768,128]{2,1,0:T(8,128)(2,1)S(1)}, bf16[2,768,128]{2,1,0:T(8,128)(2,1)S(1)}, u32[]{:S(2)}, u32[]{:S(2)}) collective-permute-start(bf16[2,768,128]{2,1,0:T(8,128)(2,1)S(1)} %get-tuple-element.12), channel_id=1, source_target_pairs={{4,0},{8,4},{12,8},{16,12},{20,16},{24,20},{28,24},{32,28},{36,32}... | collective-permute-start | bytes 1179656 | tf_op jit(solution)/shard_map/halo_back/ppermute | solution.py:354

commit v3 on v2

--- a/solution.py
+++ b/solution.py
@@ -112,9 +112,9 @@
 
 def places(block):
     return (
-        pl.ds(pl.multiple_of(block * BLOCK, BLOCK), 2 * BLOCK),
-        pl.ds(pl.multiple_of(block * HALF, HALF), 2 * HALF),
-        pl.ds(pl.multiple_of(block * QUARTER, QUARTER), 4 * QUARTER),
+        pl.ds(block * BLOCK, 2 * BLOCK),
+        pl.ds(block * HALF, 2 * HALF),
+        pl.ds(block * QUARTER, 4 * QUARTER),
     )
 
 
@@ -127,17 +127,6 @@
     per_block = BLOCK // rows
     for part in range(per_block):
         out[step * per_block + part, which, inner] = value[part * rows : (part + 1) * rows]
-
-
-def each_block(moved, one_block):
-    blocks, local, _, _ = sizes(moved)
-
-    def steps(step, carry):
-        for inner in range(local):
-            one_block(step, inner, step * local + inner)
-        return carry
-
-    lax.fori_loop(0, blocks // local, steps, 0)
 
 
 def pooled_rows(matrix, tokens):
@@ -202,6 +191,15 @@
             rext[kv, (block + 7) * QUARTER : (block + 8) * QUARTER] = pooled[HALF:]
 
 
+def without_absent(piece, block, offset, rows, is_first):
+    count = min(max(offset - block, 0) * rows, BLOCK)
+    if count == 0:
+        return piece
+    row = lax.broadcasted_iota(jnp.int32, (count, BLOCK), 0)
+    masked = jnp.where(row < is_first * count, NEG, piece[:count])
+    return masked if count == BLOCK else jnp.concatenate([masked, piece[count:]], axis=0)
+
+
 def attend_body(
     first_group,
     moved,
@@ -217,7 +215,7 @@
     mgrad,
     rgrad,
 ):
-    blocks, local, per_block, rows = sizes(moved)
+    blocks, local, _, _ = sizes(moved)
     extend(moved_kv, halo, fext, mext, rext)
     fgrad[...] = jnp.zeros_like(fgrad)
     mgrad[...] = jnp.zeros_like(mgrad)
@@ -225,48 +223,59 @@
     is_first = first_group[0]
     extended = (fext, mext, rext)
 
-    def one_block(step, inner, block):
-        queries = tokens_of(moved, 0, step, inner)
-        cotangent = tokens_of(moved, 1, step, inner)
-        keyset = window(extended, 0, block)
-        valset = window(extended, 1, block)
-        scores = dot_nt(keyset, queries)
+    def products(block):
+        queries = tokens_of(moved, 0, block // local, block % local)
+        cotangent = tokens_of(moved, 1, block // local, block % local)
+        scores = dot_nt(window(extended, 0, block), queries)
+        dweights = dot_nt(window(extended, 1, block), cotangent)
+        return queries, cotangent, scores, dweights
+
+    def softmax(block, queries, cotangent, scores, dweights):
         row = lax.broadcasted_iota(jnp.int32, (BLOCK, BLOCK), 0)
         col = lax.broadcasted_iota(jnp.int32, (BLOCK, BLOCK), 1)
-        absent = is_first * jnp.maximum(1 - block, 0) * BLOCK
-        absent_mid = is_first * jnp.maximum(3 - block, 0) * HALF
-        absent_far = is_first * jnp.maximum(7 - block, 0) * QUARTER
         scores = jnp.concatenate(
             [
-                jnp.where(row < absent, NEG, scores[:BLOCK]),
+                without_absent(scores[:BLOCK], block, 1, BLOCK, is_first),
                 jnp.where(row <= col, scores[BLOCK : 2 * BLOCK], NEG),
-                jnp.where(row < absent_mid, NEG, scores[2 * BLOCK : 3 * BLOCK]),
-                jnp.where(row < absent_far, NEG, scores[3 * BLOCK :]),
+                without_absent(scores[2 * BLOCK : 3 * BLOCK], block, 3, HALF, is_first),
+                without_absent(scores[3 * BLOCK :], block, 7, QUARTER, is_first),
             ],
             axis=0,
         )
         top = jnp.max(scores, axis=0, keepdims=True)
         powers = jnp.exp2((scores - top) * (SCALE * LOG2E))
         norm = 1.0 / jnp.sum(powers, axis=0, keepdims=True)
-        normed = powers * norm
-        weights = normed.astype(jnp.bfloat16)
-        attended = dot_tn(valset, weights)
-        turned = jnp.transpose(cotangent.astype(jnp.float32))
-        delta = jnp.sum(attended * turned, axis=0, keepdims=True)
-        dweights = dot_nt(valset, cotangent)
-        dscores = (normed * (dweights - delta)).astype(jnp.bfloat16)
-        dqueries = dot_tn(keyset, dscores) * SCALE
+        delta = jnp.sum(powers * dweights, axis=0, keepdims=True) * norm
+        weights = powers * norm
+        dscores = weights * (dweights - delta)
+        return queries, cotangent, weights.astype(jnp.bfloat16), dscores.astype(jnp.bfloat16)
+
+    def results(block, queries, cotangent, weights, dscores):
+        step, inner = block // local, block % local
+        attended = dot_tn(window(extended, 1, block), weights)
+        dqueries = dot_tn(window(extended, 0, block), dscores) * SCALE
+        store_rows(out, 0, step, inner, jnp.transpose(attended).astype(jnp.bfloat16))
+        store_rows(out, 1, step, inner, jnp.transpose(dqueries).astype(jnp.bfloat16))
         dkeys = dot_nn(dscores, queries) * SCALE
         dvalues = dot_nn(weights, cotangent)
-        store_rows(out, 0, step, inner, jnp.transpose(attended).astype(jnp.bfloat16))
-        store_rows(out, 1, step, inner, jnp.transpose(dqueries).astype(jnp.bfloat16))
         fine_at, mid_at, far_at = places(block)
         for kv, grads in enumerate((dkeys, dvalues)):
             fgrad[kv, fine_at] += grads[: 2 * BLOCK]
             mgrad[kv, mid_at] += grads[2 * BLOCK : 3 * BLOCK]
             rgrad[kv, far_at] += grads[3 * BLOCK :]
 
-    each_block(moved, one_block)
+    ahead = products(0)
+    behind = None
+    for block in range(blocks):
+        current = ahead
+        if block + 1 < blocks:
+            ahead = products(block + 1)
+        finished = softmax(block, *current)
+        if behind is not None:
+            results(block - 1, *behind)
+        behind = finished
+    results(blocks - 1, *behind)
+
     for kv in range(2):
         pairs = mgrad[kv, 2 * HALF :] * 0.5
         fours = rgrad[kv, 6 * QUARTER :] * 0.25

time: 104 us -> 98 us (0.942)
  Pallas kernels: 21.8 us -> 15.7 us
    pallas_call x1, Pallas kernels: 14.5 us -> 8.37 us  [attend(): pl.pallas_call(attend_body, out_shape=(jax.ShapeDtypeStruct((moved.shape[...]
where the time goes in v3:
time: 98 us; the launch traced here: 97.6 us
  blocking collectives  30.8 us (31%)
  waiting for transfers between devices  27.8 us (28%)
  starting transfers between devices  22.6 us (23%)
  Pallas kernels  15.7 us (16%)
    all_to_all x1, blocking collectives, exchange(): lax.all_to_all(parts, GROUP_AXES, split_axis=0, concat_axis=0, tiled=True)  30.8 us
    all_to_all x2, waiting for transfers between devices, exchange(): lax.all_to_all(parts, GROUP_AXES, split_axis=0, concat_axis=0, tiled=True)  15.5 us
    ppermute x2, waiting for transfers between devices, shifted(): return lax.ppermute(block, 'seq', route)  12.4 us
    ppermute x2, starting transfers between devices, shifted(): return lax.ppermute(block, 'seq', route)  11.9 us
    all_to_all x2, starting transfers between devices, exchange(): lax.all_to_all(parts, GROUP_AXES, split_axis=0, concat_axis=0, tiled=True)  10.7 us
    pallas_call x1, Pallas kernels, attend(): pl.pallas_call(attend_body, out_shape=(jax.ShapeDtypeStruct((moved.shape[...  8.37 us
    pallas_call x2, Pallas kernels, spread(): pl.pallas_call(spread_body, out_shape=jax.ShapeDtypeStruct((heads, count,...  4.55 us
  transfers between devices with their start and end apart: 4, of which 4 were waited for; matrix products, arithmetic and copies ran while one was open for 0% of the time, Pallas kernels for 3%

profile of v3, /device:TPU:33, one launch (start us, length us, event | category | flops | bytes accessed | tf_op | source)
XLA Modules:
  0.0 97.6 jit_solution(3815095717539941789)
XLA Ops:
  0.6 2.3 %keys_in.1 = bf16[16,2,2,64,128]{4,3,2,1,0:T(8,128)(2,1)} custom-call(bf16[2,64,2048]{2,1,0:T(8,128)(2,1)} %refs_0_.3, bf16[2,64,2048]{2,1,0:T(8,128)(2,1)} %refs_1_.3), custom_call_target="tpu_custom_call" | custom-call | bytes 2097152 | tf_op jit(solution)/shard_map/keys_in/pallas_call | solution.py:60
  2.9 6.8 %all-to-all-start = ((bf16[16,2,2,64,128]{4,3,2,1,0:T(8,128)(2,1)}), bf16[16,2,2,64,128]{4,3,2,1,0:T(8,128)(2,1)S(1)}, u32[]{:S(2)}, u32[]{:S(2)}) async-start(bf16[16,2,2,64,128]{4,3,2,1,0:T(8,128)(2,1)} %keys_in.1), calls=%async_computation | async-start | bytes 2097152 | tf_op jit(solution)/shard_map/keys_in/all_to_all | solution.py:357
  9.7 2.2 %queries_in.1 = bf16[16,2,2,64,128]{4,3,2,1,0:T(8,128)(2,1)} custom-call(bf16[2,64,2048]{2,1,0:T(8,128)(2,1)} %refs_0_.2, bf16[2,64,2048]{2,1,0:T(8,128)(2,1)} %refs_1_.2), custom_call_target="tpu_custom_call" | custom-call | bytes 2097152 | tf_op jit(solution)/shard_map/queries_in/pallas_call | solution.py:60
  12.0 13.3 %all-to-all-done.moved.moved_kv = bf16[16,2,2,64,128]{4,3,2,1,0:T(8,128)(2,1)S(1)} async-done(((bf16[16,2,2,64,128]{4,3,2,1,0:T(8,128)(2,1)}), bf16[16,2,2,64,128]{4,3,2,1,0:T(8,128)(2,1)S(1)}, u32[]{:S(2)}, u32[]{:S(2)}) %all-to-all-start) | async-done | bytes 1048608 | tf_op jit(solution)/shard_map/keys_in/all_to_all | solution.py:357
  25.2 4.0 %all-to-all-start.1 = ((bf16[16,2,2,64,128]{4,3,2,1,0:T(8,128)(2,1)}), bf16[16,2,2,64,128]{4,3,2,1,0:T(8,128)(2,1)S(1)}, u32[]{:S(2)}, u32[]{:S(2)}) async-start(bf16[16,2,2,64,128]{4,3,2,1,0:T(8,128)(2,1)} %queries_in.1), calls=%async_computation.1 | async-start | bytes 2097152 | tf_op jit(solution)/shard_map/queries_in/all_to_all | solution.py:357
  29.2 0.5 halo.1
  29.7 6.3 %collective-permute-start = (bf16[2,896,128]{2,1,0:T(8,128)(2,1)S(1)}, bf16[2,896,128]{2,1,0:T(8,128)(2,1)S(1)}, u32[]{:S(2)}, u32[]{:S(2)}) collective-permute-start(bf16[2,896,128]{2,1,0:T(8,128)(2,1)S(1)} %halo.1), channel_id=1, source_target_pairs={{0,4},{4,8},{8,12},{12,16},{16,20},{20,24},{24,28},{28,32},{32,36}... | collective-permute-start | bytes 1376264 | tf_op jit(solution)/shard_map/halo/ppermute | solution.py:363
  35.9 5.4 %collective-permute-done.halo = bf16[2,896,128]{2,1,0:T(8,128)(2,1)S(1)} collective-permute-done((bf16[2,896,128]{2,1,0:T(8,128)(2,1)S(1)}, bf16[2,896,128]{2,1,0:T(8,128)(2,1)S(1)}, u32[]{:S(2)}, u32[]{:S(2)}) %collective-permute-start) | collective-permute-done | bytes 458784 | tf_op jit(solution)/shard_map/halo/ppermute | solution.py:363
  41.3 2.2 %all-to-all-done.1.moved = bf16[16,2,2,64,128]{4,3,2,1,0:T(8,128)(2,1)S(1)} async-done(((bf16[16,2,2,64,128]{4,3,2,1,0:T(8,128)(2,1)}), bf16[16,2,2,64,128]{4,3,2,1,0:T(8,128)(2,1)S(1)}, u32[]{:S(2)}, u32[]{:S(2)}) %all-to-all-start.1) | async-done | bytes 1048608 | tf_op jit(solution)/shard_map/queries_in/all_to_all | solution.py:357
  43.5 8.4 %attend.1 = (bf16[16,4,2,64,128]{4,3,2,1,0:T(8,128)(2,1)S(1)}, f32[2,2048,128]{2,1,0:T(8,128)S(1)}, bf16[2,768,128]{2,1,0:T(8,128)(2,1)S(1)}) custom-call(s32[1]{0:T(128)} %bitcast.first_group, bf16[16,2,2,64,128]{4,3,2,1,0:T(8,128)(2,1)S(1)} %all-to-all-done.1.moved, bf16[16,2,2,64,128]{4,3,2,1,0:T(8,128)(2,1)S(1)} %all-to-all-done.moved.moved_kv, ...), custom_call_target="tpu_custom_call" | custom-call | flops 3221225472 | bytes 8388608 | tf_op jit(solution)/shard_map/attend/pallas_call | solution.py:298
  51.9 5.6 %collective-permute-start.1 = (bf16[2,768,128]{2,1,0:T(8,128)(2,1)S(1)}, bf16[2,768,128]{2,1,0:T(8,128)(2,1)S(1)}, u32[]{:S(2)}, u32[]{:S(2)}) collective-permute-start(bf16[2,768,128]{2,1,0:T(8,128)(2,1)S(1)} %get-tuple-element.12), channel_id=1, source_target_pairs={{4,0},{8,4},{12,8},{16,12},{20,16},{24,20},{28,24},{32,28},{36,32}... | collective-permute-start | bytes 1179656 | tf_op jit(solution)/shard_map/halo_back/ppermute | solution.py:363
  57.6 7.0 %collective-permute-done.1.back = bf16[2,768,128]{2,1,0:T(8,128)(2,1)S(1)} collective-permute-done((bf16[2,768,128]{2,1,0:T(8,128)(2,1)S(1)}, bf16[2,768,128]{2,1,0:T(8,128)(2,1)S(1)}, u32[]{:S(2)}, u32[]{:S(2)}) %collective-permute-start.1) | collective-permute-done | bytes 393248 | tf_op jit(solution)/shard_map/halo_back/ppermute | solution.py:363
  64.5 0.4 halo_back.1
  65.0 30.8 %all_to_all.15.moved = bf16[16,4,2,64,128]{4,3,2,1,0:T(8,128)(2,1)S(1)} all-to-all(bf16[16,4,2,64,128]{4,3,2,1,0:T(8,128)(2,1)S(1)} %halo_back.1), channel_id=1, replica_groups=mesh['head'=4,'seq'=16,'ctx'=4] {'ctx','head'}, dimensions={0} | all-to-all | bytes 4194304 | tf_op jit(solution)/shard_map/outputs/all_to_all | solution.py:357
  95.8 1.9 %outputs.1 = (bf16[2,64,2048]{2,1,0:T(8,128)(2,1)}, bf16[2,64,2048]{2,1,0:T(8,128)(2,1)}, bf16[2,64,2048]{2,1,0:T(8,128)(2,1)}, bf16[2,64,2048]{2,1,0:T(8,128)(2,1)}) custom-call(bf16[16,4,2,64,128]{4,3,2,1,0:T(8,128)(2,1)S(1)} %all_to_all.15.moved), custom_call_target="tpu_custom_call" | custom-call | bytes 4194304 | tf_op jit(solution)/shard_map/outputs/pallas_call | solution.py:81
Async XLA Ops:
  2.9 22.3 %all-to-all-start = ((bf16[16,2,2,64,128]{4,3,2,1,0:T(8,128)(2,1)}), bf16[16,2,2,64,128]{4,3,2,1,0:T(8,128)(2,1)S(1)}, u32[]{:S(2)}, u32[]{:S(2)}) async-start(bf16[16,2,2,64,128]{4,3,2,1,0:T(8,128)(2,1)} %keys_in.1), calls=%async_computation | async-start | bytes 2097152 | tf_op jit(solution)/shard_map/keys_in/all_to_all | solution.py:357
  25.2 18.3 %all-to-all-start.1 = ((bf16[16,2,2,64,128]{4,3,2,1,0:T(8,128)(2,1)}), bf16[16,2,2,64,128]{4,3,2,1,0:T(8,128)(2,1)S(1)}, u32[]{:S(2)}, u32[]{:S(2)}) async-start(bf16[16,2,2,64,128]{4,3,2,1,0:T(8,128)(2,1)} %queries_in.1), calls=%async_computation.1 | async-start | bytes 2097152 | tf_op jit(solution)/shard_map/queries_in/all_to_all | solution.py:357
  29.7 11.7 %collective-permute-start = (bf16[2,896,128]{2,1,0:T(8,128)(2,1)S(1)}, bf16[2,896,128]{2,1,0:T(8,128)(2,1)S(1)}, u32[]{:S(2)}, u32[]{:S(2)}) collective-permute-start(bf16[2,896,128]{2,1,0:T(8,128)(2,1)S(1)} %halo.1), channel_id=1, source_target_pairs={{0,4},{4,8},{8,12},{12,16},{16,20},{20,24},{24,28},{28,32},{32,36}... | collective-permute-start | bytes 1376264 | tf_op jit(solution)/shard_map/halo/ppermute | solution.py:363
  51.9 12.6 %collective-permute-start.1 = (bf16[2,768,128]{2,1,0:T(8,128)(2,1)S(1)}, bf16[2,768,128]{2,1,0:T(8,128)(2,1)S(1)}, u32[]{:S(2)}, u32[]{:S(2)}) collective-permute-start(bf16[2,768,128]{2,1,0:T(8,128)(2,1)S(1)} %get-tuple-element.12), channel_id=1, source_target_pairs={{4,0},{8,4},{12,8},{16,12},{20,16},{24,20},{28,24},{32,28},{36,32}... | collective-permute-start | bytes 1179656 | tf_op jit(solution)/shard_map/halo_back/ppermute | solution.py:363

commit v4 on v3

--- a/solution.py
+++ b/solution.py
@@ -318,6 +318,7 @@
 
 
 def finish_body(total, back, given, out, scratch):
+    out[:, :2] = given[:, :2]
     sources, _, local, rows, _ = out.shape
     per_block = BLOCK // rows
     blocks = sources // per_block * local

time: 98 us -> 98.1 us (level)
  no operation moved by 1% of the time
where the time goes in v4:
time: 98.1 us; the launch traced here: 97.7 us
  blocking collectives  30.8 us (31%)
  waiting for transfers between devices  27.8 us (28%)
  starting transfers between devices  22.6 us (23%)
  Pallas kernels  15.8 us (16%)
    all_to_all x1, blocking collectives, exchange(): lax.all_to_all(parts, GROUP_AXES, split_axis=0, concat_axis=0, tiled=True)  30.8 us
    all_to_all x2, waiting for transfers between devices, exchange(): lax.all_to_all(parts, GROUP_AXES, split_axis=0, concat_axis=0, tiled=True)  15.5 us
    ppermute x2, waiting for transfers between devices, shifted(): return lax.ppermute(block, 'seq', route)  12.4 us
    ppermute x2, starting transfers between devices, shifted(): return lax.ppermute(block, 'seq', route)  11.9 us
    all_to_all x2, starting transfers between devices, exchange(): lax.all_to_all(parts, GROUP_AXES, split_axis=0, concat_axis=0, tiled=True)  10.7 us
    pallas_call x1, Pallas kernels, attend(): pl.pallas_call(attend_body, out_shape=(jax.ShapeDtypeStruct((moved.shape[...  8.37 us
    pallas_call x2, Pallas kernels, spread(): pl.pallas_call(spread_body, out_shape=jax.ShapeDtypeStruct((heads, count,...  4.55 us
  transfers between devices with their start and end apart: 4, of which 4 were waited for; matrix products, arithmetic and copies ran while one was open for 0% of the time, Pallas kernels for 3%

profile of v4, /device:TPU:33, one launch (start us, length us, event | category | flops | bytes accessed | tf_op | source)
XLA Modules:
  0.0 97.7 jit_solution(17704485325443270682)
XLA Ops:
  0.6 2.3 %keys_in.1 = bf16[16,2,2,64,128]{4,3,2,1,0:T(8,128)(2,1)} custom-call(bf16[2,64,2048]{2,1,0:T(8,128)(2,1)} %refs_0_.3, bf16[2,64,2048]{2,1,0:T(8,128)(2,1)} %refs_1_.3), custom_call_target="tpu_custom_call" | custom-call | bytes 2097152 | tf_op jit(solution)/shard_map/keys_in/pallas_call | solution.py:60
  2.9 6.8 %all-to-all-start = ((bf16[16,2,2,64,128]{4,3,2,1,0:T(8,128)(2,1)}), bf16[16,2,2,64,128]{4,3,2,1,0:T(8,128)(2,1)S(1)}, u32[]{:S(2)}, u32[]{:S(2)}) async-start(bf16[16,2,2,64,128]{4,3,2,1,0:T(8,128)(2,1)} %keys_in.1), calls=%async_computation | async-start | bytes 2097152 | tf_op jit(solution)/shard_map/keys_in/all_to_all | solution.py:358
  9.7 2.2 %queries_in.1 = bf16[16,2,2,64,128]{4,3,2,1,0:T(8,128)(2,1)} custom-call(bf16[2,64,2048]{2,1,0:T(8,128)(2,1)} %refs_0_.2, bf16[2,64,2048]{2,1,0:T(8,128)(2,1)} %refs_1_.2), custom_call_target="tpu_custom_call" | custom-call | bytes 2097152 | tf_op jit(solution)/shard_map/queries_in/pallas_call | solution.py:60
  12.0 13.3 %all-to-all-done.moved.moved_kv = bf16[16,2,2,64,128]{4,3,2,1,0:T(8,128)(2,1)S(1)} async-done(((bf16[16,2,2,64,128]{4,3,2,1,0:T(8,128)(2,1)}), bf16[16,2,2,64,128]{4,3,2,1,0:T(8,128)(2,1)S(1)}, u32[]{:S(2)}, u32[]{:S(2)}) %all-to-all-start) | async-done | bytes 1048608 | tf_op jit(solution)/shard_map/keys_in/all_to_all | solution.py:358
  25.2 4.0 %all-to-all-start.1 = ((bf16[16,2,2,64,128]{4,3,2,1,0:T(8,128)(2,1)}), bf16[16,2,2,64,128]{4,3,2,1,0:T(8,128)(2,1)S(1)}, u32[]{:S(2)}, u32[]{:S(2)}) async-start(bf16[16,2,2,64,128]{4,3,2,1,0:T(8,128)(2,1)} %queries_in.1), calls=%async_computation.1 | async-start | bytes 2097152 | tf_op jit(solution)/shard_map/queries_in/all_to_all | solution.py:358
  29.2 0.5 halo.1
  29.7 6.3 %collective-permute-start = (bf16[2,896,128]{2,1,0:T(8,128)(2,1)S(1)}, bf16[2,896,128]{2,1,0:T(8,128)(2,1)S(1)}, u32[]{:S(2)}, u32[]{:S(2)}) collective-permute-start(bf16[2,896,128]{2,1,0:T(8,128)(2,1)S(1)} %halo.1), channel_id=1, source_target_pairs={{0,4},{4,8},{8,12},{12,16},{16,20},{20,24},{24,28},{28,32},{32,36}... | collective-permute-start | bytes 1376264 | tf_op jit(solution)/shard_map/halo/ppermute | solution.py:364
  35.9 5.4 %collective-permute-done.halo = bf16[2,896,128]{2,1,0:T(8,128)(2,1)S(1)} collective-permute-done((bf16[2,896,128]{2,1,0:T(8,128)(2,1)S(1)}, bf16[2,896,128]{2,1,0:T(8,128)(2,1)S(1)}, u32[]{:S(2)}, u32[]{:S(2)}) %collective-permute-start) | collective-permute-done | bytes 458784 | tf_op jit(solution)/shard_map/halo/ppermute | solution.py:364
  41.3 2.2 %all-to-all-done.1.moved = bf16[16,2,2,64,128]{4,3,2,1,0:T(8,128)(2,1)S(1)} async-done(((bf16[16,2,2,64,128]{4,3,2,1,0:T(8,128)(2,1)}), bf16[16,2,2,64,128]{4,3,2,1,0:T(8,128)(2,1)S(1)}, u32[]{:S(2)}, u32[]{:S(2)}) %all-to-all-start.1) | async-done | bytes 1048608 | tf_op jit(solution)/shard_map/queries_in/all_to_all | solution.py:358
  43.5 8.4 %attend.1 = (bf16[16,4,2,64,128]{4,3,2,1,0:T(8,128)(2,1)S(1)}, f32[2,2048,128]{2,1,0:T(8,128)S(1)}, bf16[2,768,128]{2,1,0:T(8,128)(2,1)S(1)}) custom-call(s32[1]{0:T(128)} %bitcast.first_group, bf16[16,2,2,64,128]{4,3,2,1,0:T(8,128)(2,1)S(1)} %all-to-all-done.1.moved, bf16[16,2,2,64,128]{4,3,2,1,0:T(8,128)(2,1)S(1)} %all-to-all-done.moved.moved_kv, ...), custom_call_target="tpu_custom_call" | custom-call | flops 3221225472 | bytes 8388608 | tf_op jit(solution)/shard_map/attend/pallas_call | solution.py:298
  51.9 5.6 %collective-permute-start.1 = (bf16[2,768,128]{2,1,0:T(8,128)(2,1)S(1)}, bf16[2,768,128]{2,1,0:T(8,128)(2,1)S(1)}, u32[]{:S(2)}, u32[]{:S(2)}) collective-permute-start(bf16[2,768,128]{2,1,0:T(8,128)(2,1)S(1)} %get-tuple-element.12), channel_id=1, source_target_pairs={{4,0},{8,4},{12,8},{16,12},{20,16},{24,20},{28,24},{32,28},{36,32}... | collective-permute-start | bytes 1179656 | tf_op jit(solution)/shard_map/halo_back/ppermute | solution.py:364
  57.6 7.0 %collective-permute-done.1.back = bf16[2,768,128]{2,1,0:T(8,128)(2,1)S(1)} collective-permute-done((bf16[2,768,128]{2,1,0:T(8,128)(2,1)S(1)}, bf16[2,768,128]{2,1,0:T(8,128)(2,1)S(1)}, u32[]{:S(2)}, u32[]{:S(2)}) %collective-permute-start.1) | collective-permute-done | bytes 393248 | tf_op jit(solution)/shard_map/halo_back/ppermute | solution.py:364
  64.5 0.6 halo_back.1
  65.1 30.8 %all_to_all.15.moved = bf16[16,4,2,64,128]{4,3,2,1,0:T(8,128)(2,1)S(1)} all-to-all(bf16[16,4,2,64,128]{4,3,2,1,0:T(8,128)(2,1)S(1)} %halo_back.1), channel_id=1, replica_groups=mesh['head'=4,'seq'=16,'ctx'=4] {'ctx','head'}, dimensions={0} | all-to-all | bytes 4194304 | tf_op jit(solution)/shard_map/outputs/all_to_all | solution.py:358
  95.9 1.9 %outputs.1 = (bf16[2,64,2048]{2,1,0:T(8,128)(2,1)}, bf16[2,64,2048]{2,1,0:T(8,128)(2,1)}, bf16[2,64,2048]{2,1,0:T(8,128)(2,1)}, bf16[2,64,2048]{2,1,0:T(8,128)(2,1)}) custom-call(bf16[16,4,2,64,128]{4,3,2,1,0:T(8,128)(2,1)S(1)} %all_to_all.15.moved), custom_call_target="tpu_custom_call" | custom-call | bytes 4194304 | tf_op jit(solution)/shard_map/outputs/pallas_call | solution.py:81
Async XLA Ops:
  2.9 22.3 %all-to-all-start = ((bf16[16,2,2,64,128]{4,3,2,1,0:T(8,128)(2,1)}), bf16[16,2,2,64,128]{4,3,2,1,0:T(8,128)(2,1)S(1)}, u32[]{:S(2)}, u32[]{:S(2)}) async-start(bf16[16,2,2,64,128]{4,3,2,1,0:T(8,128)(2,1)} %keys_in.1), calls=%async_computation | async-start | bytes 2097152 | tf_op jit(solution)/shard_map/keys_in/all_to_all | solution.py:358
  25.2 18.3 %all-to-all-start.1 = ((bf16[16,2,2,64,128]{4,3,2,1,0:T(8,128)(2,1)}), bf16[16,2,2,64,128]{4,3,2,1,0:T(8,128)(2,1)S(1)}, u32[]{:S(2)}, u32[]{:S(2)}) async-start(bf16[16,2,2,64,128]{4,3,2,1,0:T(8,128)(2,1)} %queries_in.1), calls=%async_computation.1 | async-start | bytes 2097152 | tf_op jit(solution)/shard_map/queries_in/all_to_all | solution.py:358
  29.7 11.7 %collective-permute-start = (bf16[2,896,128]{2,1,0:T(8,128)(2,1)S(1)}, bf16[2,896,128]{2,1,0:T(8,128)(2,1)S(1)}, u32[]{:S(2)}, u32[]{:S(2)}) collective-permute-start(bf16[2,896,128]{2,1,0:T(8,128)(2,1)S(1)} %halo.1), channel_id=1, source_target_pairs={{0,4},{4,8},{8,12},{12,16},{16,20},{20,24},{24,28},{28,32},{32,36}... | collective-permute-start | bytes 1376264 | tf_op jit(solution)/shard_map/halo/ppermute | solution.py:364
  51.9 12.6 %collective-permute-start.1 = (bf16[2,768,128]{2,1,0:T(8,128)(2,1)S(1)}, bf16[2,768,128]{2,1,0:T(8,128)(2,1)S(1)}, u32[]{:S(2)}, u32[]{:S(2)}) collective-permute-start(bf16[2,768,128]{2,1,0:T(8,128)(2,1)S(1)} %get-tuple-element.12), channel_id=1, source_target_pairs={{4,0},{8,4},{12,8},{16,12},{20,16},{24,20},{28,24},{32,28},{36,32}... | collective-permute-start | bytes 1179656 | tf_op jit(solution)/shard_map/halo_back/ppermute | solution.py:364

commit v5 on v4

--- a/solution.py
+++ b/solution.py
@@ -211,15 +211,12 @@
     fext,
     mext,
     rext,
-    fgrad,
+    edge,
     mgrad,
     rgrad,
 ):
     blocks, local, _, _ = sizes(moved)
     extend(moved_kv, halo, fext, mext, rext)
-    fgrad[...] = jnp.zeros_like(fgrad)
-    mgrad[...] = jnp.zeros_like(mgrad)
-    rgrad[...] = jnp.zeros_like(rgrad)
     is_first = first_group[0]
     extended = (fext, mext, rext)
 
@@ -258,11 +255,20 @@
         store_rows(out, 1, step, inner, jnp.transpose(dqueries).astype(jnp.bfloat16))
         dkeys = dot_nn(dscores, queries) * SCALE
         dvalues = dot_nn(weights, cotangent)
-        fine_at, mid_at, far_at = places(block)
         for kv, grads in enumerate((dkeys, dvalues)):
-            fgrad[kv, fine_at] += grads[: 2 * BLOCK]
-            mgrad[kv, mid_at] += grads[2 * BLOCK : 3 * BLOCK]
-            rgrad[kv, far_at] += grads[3 * BLOCK :]
+            before, here = grads[:BLOCK], grads[BLOCK : 2 * BLOCK]
+            pairs, fours = grads[2 * BLOCK : 3 * BLOCK], grads[3 * BLOCK :]
+            total[kv, block * BLOCK : (block + 1) * BLOCK] = here
+            if block == 0:
+                edge[kv] = before
+                mgrad[kv, : 2 * HALF] = pairs
+                rgrad[kv, : 4 * QUARTER] = fours
+                continue
+            total[kv, (block - 1) * BLOCK : block * BLOCK] += before
+            mgrad[kv, block * HALF : (block + 1) * HALF] += pairs[:HALF]
+            mgrad[kv, (block + 1) * HALF : (block + 2) * HALF] = pairs[HALF:]
+            rgrad[kv, block * QUARTER : (block + 3) * QUARTER] += fours[: 3 * QUARTER]
+            rgrad[kv, (block + 3) * QUARTER : (block + 4) * QUARTER] = fours[3 * QUARTER :]
 
     ahead = products(0)
     behind = None
@@ -278,16 +284,17 @@
 
     for kv in range(2):
         pairs = mgrad[kv, 2 * HALF :] * 0.5
+        for lane in range(2):
+            edge[kv, pl.ds(lane, HALF, stride=2), :] += pairs[:HALF]
+            total[kv, pl.ds(lane, (blocks - 2) * HALF, stride=2), :] += pairs[HALF:]
         fours = rgrad[kv, 6 * QUARTER :] * 0.25
-        for lane in range(2):
-            fgrad[kv, pl.ds(lane, (blocks + 1) * HALF, stride=2), :] += pairs
         for lane in range(4):
-            fgrad[kv, pl.ds(lane, (blocks + 1) * QUARTER, stride=4), :] += fours
+            edge[kv, pl.ds(lane, QUARTER, stride=4), :] += fours[:QUARTER]
+            total[kv, pl.ds(lane, (blocks - 4) * QUARTER, stride=4), :] += fours[QUARTER:]
         shares = rgrad[kv, 4 * QUARTER : 6 * QUARTER] * 0.5
         for lane in range(2):
             mgrad[kv, pl.ds(lane, 2 * QUARTER, stride=2), :] += shares
-        total[kv] = fgrad[kv, BLOCK:]
-        back[kv, :BLOCK] = fgrad[kv, :BLOCK].astype(jnp.bfloat16)
+        back[kv, :BLOCK] = edge[kv].astype(jnp.bfloat16)
         back[kv, BLOCK : BLOCK + 2 * HALF] = mgrad[kv, : 2 * HALF].astype(jnp.bfloat16)
         back[kv, BLOCK + 2 * HALF :] = rgrad[kv, : 4 * QUARTER].astype(jnp.bfloat16)
 
@@ -308,9 +315,9 @@
             pltpu.VMEM((2, (blocks + 1) * BLOCK, HD), jnp.bfloat16),
             pltpu.VMEM((2, (blocks + 3) * HALF, HD), jnp.bfloat16),
             pltpu.VMEM((2, (blocks + 7) * QUARTER, HD), jnp.bfloat16),
-            pltpu.VMEM((2, (blocks + 1) * BLOCK, HD), f32),
-            pltpu.VMEM((2, (blocks + 3) * HALF, HD), f32),
-            pltpu.VMEM((2, (blocks + 7) * QUARTER, HD), f32),
+            pltpu.VMEM((2, BLOCK, HD), f32),
+            pltpu.VMEM((2, (blocks + 1) * HALF, HD), f32),
+            pltpu.VMEM((2, (blocks + 3) * QUARTER, HD), f32),
         ],
         compiler_params=params(24),
         cost_estimate=cost(blocks * 12 * BLOCK * 4 * BLOCK * HD, 8 * 2**20),

time: 98.1 us -> 97.9 us (level)
  no operation moved by 1% of the time
where the time goes in v5:
time: 97.9 us; the launch traced here: 97.5 us
  blocking collectives  30.8 us (31%)
  waiting for transfers between devices  27.8 us (28%)
  starting transfers between devices  22.6 us (23%)
  Pallas kernels  15.6 us (16%)
    all_to_all x1, blocking collectives, exchange(): lax.all_to_all(parts, GROUP_AXES, split_axis=0, concat_axis=0, tiled=True)  30.8 us
    all_to_all x2, waiting for transfers between devices, exchange(): lax.all_to_all(parts, GROUP_AXES, split_axis=0, concat_axis=0, tiled=True)  15.5 us
    ppermute x2, waiting for transfers between devices, shifted(): return lax.ppermute(block, 'seq', route)  12.4 us
    ppermute x2, starting transfers between devices, shifted(): return lax.ppermute(block, 'seq', route)  11.9 us
    all_to_all x2, starting transfers between devices, exchange(): lax.all_to_all(parts, GROUP_AXES, split_axis=0, concat_axis=0, tiled=True)  10.7 us
    pallas_call x1, Pallas kernels, attend(): pl.pallas_call(attend_body, out_shape=(jax.ShapeDtypeStruct((moved.shape[...  8.12 us
    pallas_call x2, Pallas kernels, spread(): pl.pallas_call(spread_body, out_shape=jax.ShapeDtypeStruct((heads, count,...  4.55 us
  transfers between devices with their start and end apart: 4, of which 4 were waited for; matrix products, arithmetic and copies ran while one was open for 0% of the time, Pallas kernels for 3%

profile of v5, /device:TPU:33, one launch (start us, length us, event | category | flops | bytes accessed | tf_op | source)
XLA Modules:
  0.0 97.5 jit_solution(12173965118637613725)
XLA Ops:
  0.6 2.3 %keys_in.1 = bf16[16,2,2,64,128]{4,3,2,1,0:T(8,128)(2,1)} custom-call(bf16[2,64,2048]{2,1,0:T(8,128)(2,1)} %refs_0_.3, bf16[2,64,2048]{2,1,0:T(8,128)(2,1)} %refs_1_.3), custom_call_target="tpu_custom_call" | custom-call | bytes 2097152 | tf_op jit(solution)/shard_map/keys_in/pallas_call | solution.py:60
  2.9 6.8 %all-to-all-start = ((bf16[16,2,2,64,128]{4,3,2,1,0:T(8,128)(2,1)}), bf16[16,2,2,64,128]{4,3,2,1,0:T(8,128)(2,1)S(1)}, u32[]{:S(2)}, u32[]{:S(2)}) async-start(bf16[16,2,2,64,128]{4,3,2,1,0:T(8,128)(2,1)} %keys_in.1), calls=%async_computation | async-start | bytes 2097152 | tf_op jit(solution)/shard_map/keys_in/all_to_all | solution.py:365
  9.7 2.2 %queries_in.1 = bf16[16,2,2,64,128]{4,3,2,1,0:T(8,128)(2,1)} custom-call(bf16[2,64,2048]{2,1,0:T(8,128)(2,1)} %refs_0_.2, bf16[2,64,2048]{2,1,0:T(8,128)(2,1)} %refs_1_.2), custom_call_target="tpu_custom_call" | custom-call | bytes 2097152 | tf_op jit(solution)/shard_map/queries_in/pallas_call | solution.py:60
  12.0 13.3 %all-to-all-done.moved.moved_kv = bf16[16,2,2,64,128]{4,3,2,1,0:T(8,128)(2,1)S(1)} async-done(((bf16[16,2,2,64,128]{4,3,2,1,0:T(8,128)(2,1)}), bf16[16,2,2,64,128]{4,3,2,1,0:T(8,128)(2,1)S(1)}, u32[]{:S(2)}, u32[]{:S(2)}) %all-to-all-start) | async-done | bytes 1048608 | tf_op jit(solution)/shard_map/keys_in/all_to_all | solution.py:365
  25.2 4.0 %all-to-all-start.1 = ((bf16[16,2,2,64,128]{4,3,2,1,0:T(8,128)(2,1)}), bf16[16,2,2,64,128]{4,3,2,1,0:T(8,128)(2,1)S(1)}, u32[]{:S(2)}, u32[]{:S(2)}) async-start(bf16[16,2,2,64,128]{4,3,2,1,0:T(8,128)(2,1)} %queries_in.1), calls=%async_computation.1 | async-start | bytes 2097152 | tf_op jit(solution)/shard_map/queries_in/all_to_all | solution.py:365
  29.2 0.5 halo.1
  29.7 6.3 %collective-permute-start = (bf16[2,896,128]{2,1,0:T(8,128)(2,1)S(1)}, bf16[2,896,128]{2,1,0:T(8,128)(2,1)S(1)}, u32[]{:S(2)}, u32[]{:S(2)}) collective-permute-start(bf16[2,896,128]{2,1,0:T(8,128)(2,1)S(1)} %halo.1), channel_id=1, source_target_pairs={{0,4},{4,8},{8,12},{12,16},{16,20},{20,24},{24,28},{28,32},{32,36}... | collective-permute-start | bytes 1376264 | tf_op jit(solution)/shard_map/halo/ppermute | solution.py:371
  35.9 5.4 %collective-permute-done.halo = bf16[2,896,128]{2,1,0:T(8,128)(2,1)S(1)} collective-permute-done((bf16[2,896,128]{2,1,0:T(8,128)(2,1)S(1)}, bf16[2,896,128]{2,1,0:T(8,128)(2,1)S(1)}, u32[]{:S(2)}, u32[]{:S(2)}) %collective-permute-start) | collective-permute-done | bytes 458784 | tf_op jit(solution)/shard_map/halo/ppermute | solution.py:371
  41.3 2.2 %all-to-all-done.1.moved = bf16[16,2,2,64,128]{4,3,2,1,0:T(8,128)(2,1)S(1)} async-done(((bf16[16,2,2,64,128]{4,3,2,1,0:T(8,128)(2,1)}), bf16[16,2,2,64,128]{4,3,2,1,0:T(8,128)(2,1)S(1)}, u32[]{:S(2)}, u32[]{:S(2)}) %all-to-all-start.1) | async-done | bytes 1048608 | tf_op jit(solution)/shard_map/queries_in/all_to_all | solution.py:365
  43.5 8.1 %attend.1 = (bf16[16,4,2,64,128]{4,3,2,1,0:T(8,128)(2,1)S(1)}, f32[2,2048,128]{2,1,0:T(8,128)S(1)}, bf16[2,768,128]{2,1,0:T(8,128)(2,1)S(1)}) custom-call(s32[1]{0:T(128)} %bitcast.first_group, bf16[16,2,2,64,128]{4,3,2,1,0:T(8,128)(2,1)S(1)} %all-to-all-done.1.moved, bf16[16,2,2,64,128]{4,3,2,1,0:T(8,128)(2,1)S(1)} %all-to-all-done.moved.moved_kv, ...), custom_call_target="tpu_custom_call" | custom-call | flops 3221225472 | bytes 8388608 | tf_op jit(solution)/shard_map/attend/pallas_call | solution.py:305
  51.7 5.6 %collective-permute-start.1 = (bf16[2,768,128]{2,1,0:T(8,128)(2,1)S(1)}, bf16[2,768,128]{2,1,0:T(8,128)(2,1)S(1)}, u32[]{:S(2)}, u32[]{:S(2)}) collective-permute-start(bf16[2,768,128]{2,1,0:T(8,128)(2,1)S(1)} %get-tuple-element.12), channel_id=1, source_target_pairs={{4,0},{8,4},{12,8},{16,12},{20,16},{24,20},{28,24},{32,28},{36,32}... | collective-permute-start | bytes 1179656 | tf_op jit(solution)/shard_map/halo_back/ppermute | solution.py:371
  57.3 7.0 %collective-permute-done.1.back = bf16[2,768,128]{2,1,0:T(8,128)(2,1)S(1)} collective-permute-done((bf16[2,768,128]{2,1,0:T(8,128)(2,1)S(1)}, bf16[2,768,128]{2,1,0:T(8,128)(2,1)S(1)}, u32[]{:S(2)}, u32[]{:S(2)}) %collective-permute-start.1) | collective-permute-done | bytes 393248 | tf_op jit(solution)/shard_map/halo_back/ppermute | solution.py:371
  64.3 0.6 halo_back.1
  64.9 30.8 %all_to_all.15.moved = bf16[16,4,2,64,128]{4,3,2,1,0:T(8,128)(2,1)S(1)} all-to-all(bf16[16,4,2,64,128]{4,3,2,1,0:T(8,128)(2,1)S(1)} %halo_back.1), channel_id=1, replica_groups=mesh['head'=4,'seq'=16,'ctx'=4] {'ctx','head'}, dimensions={0} | all-to-all | bytes 4194304 | tf_op jit(solution)/shard_map/outputs/all_to_all | solution.py:365
  95.6 1.9 %outputs.1 = (bf16[2,64,2048]{2,1,0:T(8,128)(2,1)}, bf16[2,64,2048]{2,1,0:T(8,128)(2,1)}, bf16[2,64,2048]{2,1,0:T(8,128)(2,1)}, bf16[2,64,2048]{2,1,0:T(8,128)(2,1)}) custom-call(bf16[16,4,2,64,128]{4,3,2,1,0:T(8,128)(2,1)S(1)} %all_to_all.15.moved), custom_call_target="tpu_custom_call" | custom-call | bytes 4194304 | tf_op jit(solution)/shard_map/outputs/pallas_call | solution.py:81
Async XLA Ops:
  2.9 22.3 %all-to-all-start = ((bf16[16,2,2,64,128]{4,3,2,1,0:T(8,128)(2,1)}), bf16[16,2,2,64,128]{4,3,2,1,0:T(8,128)(2,1)S(1)}, u32[]{:S(2)}, u32[]{:S(2)}) async-start(bf16[16,2,2,64,128]{4,3,2,1,0:T(8,128)(2,1)} %keys_in.1), calls=%async_computation | async-start | bytes 2097152 | tf_op jit(solution)/shard_map/keys_in/all_to_all | solution.py:365
  25.2 18.3 %all-to-all-start.1 = ((bf16[16,2,2,64,128]{4,3,2,1,0:T(8,128)(2,1)}), bf16[16,2,2,64,128]{4,3,2,1,0:T(8,128)(2,1)S(1)}, u32[]{:S(2)}, u32[]{:S(2)}) async-start(bf16[16,2,2,64,128]{4,3,2,1,0:T(8,128)(2,1)} %queries_in.1), calls=%async_computation.1 | async-start | bytes 2097152 | tf_op jit(solution)/shard_map/queries_in/all_to_all | solution.py:365
  29.7 11.7 %collective-permute-start = (bf16[2,896,128]{2,1,0:T(8,128)(2,1)S(1)}, bf16[2,896,128]{2,1,0:T(8,128)(2,1)S(1)}, u32[]{:S(2)}, u32[]{:S(2)}) collective-permute-start(bf16[2,896,128]{2,1,0:T(8,128)(2,1)S(1)} %halo.1), channel_id=1, source_target_pairs={{0,4},{4,8},{8,12},{12,16},{16,20},{20,24},{24,28},{28,32},{32,36}... | collective-permute-start | bytes 1376264 | tf_op jit(solution)/shard_map/halo/ppermute | solution.py:371
  51.7 12.6 %collective-permute-start.1 = (bf16[2,768,128]{2,1,0:T(8,128)(2,1)S(1)}, bf16[2,768,128]{2,1,0:T(8,128)(2,1)S(1)}, u32[]{:S(2)}, u32[]{:S(2)}) collective-permute-start(bf16[2,768,128]{2,1,0:T(8,128)(2,1)S(1)} %get-tuple-element.12), channel_id=1, source_target_pairs={{4,0},{8,4},{12,8},{16,12},{20,16},{24,20},{28,24},{32,28},{36,32}... | collective-permute-start | bytes 1179656 | tf_op jit(solution)/shard_map/halo_back/ppermute | solution.py:371

commit v6 on v5

--- a/solution.py
+++ b/solution.py
@@ -36,53 +36,66 @@
 
 
 def spread_body(*refs):
-    count = (len(refs) - 2) // 2
-    sources, out, held, sems = refs[:count], refs[count], refs[count + 1 : -1], refs[-1]
-    blocks = out.shape[2]
-    copies = {}
+    count = (len(refs) - 2) // 3
+    sources, out = refs[:count], refs[count]
+    held, turned, sems = refs[count + 1 : 2 * count + 1], refs[2 * count + 1 : -1], refs[-1]
+    heads, _, blocks, _, _ = out.shape
+    fetches = {}
     for which in range(count):
         for block in range(blocks):
-            copies[which, block] = pltpu.make_async_copy(
+            fetches[which, block] = pltpu.make_async_copy(
                 sources[which].at[block], held[which].at[block], sems.at[which, block]
             )
-            copies[which, block].start()
+            fetches[which, block].start()
+    sends = []
     for which in range(count):
         for block in range(blocks):
-            copies[which, block].wait()
-            for head in range(out.shape[0]):
-                out[head, which, block] = held[which][block, :, head * HD : (head + 1) * HD]
+            fetches[which, block].wait()
+            for head in range(heads):
+                turned[which][head, block] = held[which][block, :, head * HD : (head + 1) * HD]
+        send = pltpu.make_async_copy(turned[which], out.at[:, which], sems.at[which, blocks])
+        send.start()
+        sends.append(send)
+    for send in sends:
+        send.wait()
 
 
 def spread(*arrays):
     blocks, rows, features = arrays[0].shape
     heads = features // HD
     count = len(arrays)
+    kind = arrays[0].dtype
+    there = pl.BlockSpec(memory_space=pltpu.HBM)
     return pl.pallas_call(
         spread_body,
-        out_shape=jax.ShapeDtypeStruct((heads, count, blocks, rows, HD), arrays[0].dtype),
-        in_specs=[pl.BlockSpec(memory_space=pltpu.HBM)] * count,
-        out_specs=whole(1)[0],
-        scratch_shapes=[pltpu.VMEM((blocks, rows, features), arrays[0].dtype)] * count
-        + [pltpu.SemaphoreType.DMA((count, blocks))],
+        out_shape=jax.ShapeDtypeStruct((heads, count, blocks, rows, HD), kind),
+        in_specs=[there] * count,
+        out_specs=there,
+        scratch_shapes=[pltpu.VMEM((blocks, rows, features), kind)] * count
+        + [pltpu.VMEM((heads, blocks, rows, HD), kind)] * count
+        + [pltpu.SemaphoreType.DMA((count, blocks + 1))],
         compiler_params=params(58),
         cost_estimate=cost(0, 4 * count * arrays[0].size),
     )(*arrays)
 
 
 def join_body(moved, *outs):
+    block = pl.program_id(0)
     for which, out in enumerate(outs):
         for head in range(moved.shape[0]):
-            out[:, :, head * HD : (head + 1) * HD] = moved[head, which]
+            out[0, :, head * HD : (head + 1) * HD] = moved[head, which, block]
 
 
 def join(moved):
     heads, count, blocks, rows, _ = moved.shape
     out = jax.ShapeDtypeStruct((blocks, rows, heads * HD), moved.dtype)
+    one = pl.BlockSpec((1, rows, heads * HD), lambda block: (block, 0, 0))
     return pl.pallas_call(
         join_body,
+        grid=(blocks,),
         out_shape=(out,) * count,
         in_specs=whole(1),
-        out_specs=tuple(whole(count)),
+        out_specs=(one,) * count,
         compiler_params=params(8),
         cost_estimate=cost(0, 4 * moved.size),
     )(moved)

time: 97.9 us -> 97.4 us (level)
  no operation moved by 1% of the time
where the time goes in v6:
time: 97.4 us; the launch traced here: 97 us
  blocking collectives  30.8 us (32%)
  waiting for transfers between devices  28 us (29%)
  starting transfers between devices  22.6 us (23%)
  Pallas kernels  14.9 us (15%)
    all_to_all x1, blocking collectives, exchange(): lax.all_to_all(parts, GROUP_AXES, split_axis=0, concat_axis=0, tiled=True)  30.8 us
    all_to_all x2, waiting for transfers between devices, exchange(): lax.all_to_all(parts, GROUP_AXES, split_axis=0, concat_axis=0, tiled=True)  15.6 us
    ppermute x2, waiting for transfers between devices, shifted(): return lax.ppermute(block, 'seq', route)  12.4 us
    ppermute x2, starting transfers between devices, shifted(): return lax.ppermute(block, 'seq', route)  11.9 us
    all_to_all x2, starting transfers between devices, exchange(): lax.all_to_all(parts, GROUP_AXES, split_axis=0, concat_axis=0, tiled=True)  10.7 us
    pallas_call x1, Pallas kernels, attend(): pl.pallas_call(attend_body, out_shape=(jax.ShapeDtypeStruct((moved.shape[...  8.13 us
    pallas_call x2, Pallas kernels, spread(): pl.pallas_call(spread_body, out_shape=jax.ShapeDtypeStruct((heads, count,...  4.29 us
  transfers between devices with their start and end apart: 4, of which 4 were waited for; matrix products, arithmetic and copies ran while one was open for 0% of the time, Pallas kernels for 3%

profile of v6, /device:TPU:33, one launch (start us, length us, event | category | flops | bytes accessed | tf_op | source)
XLA Modules:
  0.0 97.0 jit_solution(11960336722937581807)
XLA Ops:
  0.6 2.2 %keys_in.1 = bf16[16,2,2,64,128]{4,3,2,1,0:T(8,128)(2,1)} custom-call(bf16[2,64,2048]{2,1,0:T(8,128)(2,1)} %refs_0_.3, bf16[2,64,2048]{2,1,0:T(8,128)(2,1)} %refs_1_.3), custom_call_target="tpu_custom_call" | custom-call | bytes 2097152 | tf_op jit(solution)/shard_map/keys_in/pallas_call | solution.py:69
  2.8 6.8 %all-to-all-start = ((bf16[16,2,2,64,128]{4,3,2,1,0:T(8,128)(2,1)}), bf16[16,2,2,64,128]{4,3,2,1,0:T(8,128)(2,1)S(1)}, u32[]{:S(2)}, u32[]{:S(2)}) async-start(bf16[16,2,2,64,128]{4,3,2,1,0:T(8,128)(2,1)} %keys_in.1), calls=%async_computation | async-start | bytes 2097152 | tf_op jit(solution)/shard_map/keys_in/all_to_all | solution.py:378
  9.6 2.1 %queries_in.1 = bf16[16,2,2,64,128]{4,3,2,1,0:T(8,128)(2,1)} custom-call(bf16[2,64,2048]{2,1,0:T(8,128)(2,1)} %refs_0_.2, bf16[2,64,2048]{2,1,0:T(8,128)(2,1)} %refs_1_.2), custom_call_target="tpu_custom_call" | custom-call | bytes 2097152 | tf_op jit(solution)/shard_map/queries_in/pallas_call | solution.py:69
  11.7 13.4 %all-to-all-done.moved.moved_kv = bf16[16,2,2,64,128]{4,3,2,1,0:T(8,128)(2,1)S(1)} async-done(((bf16[16,2,2,64,128]{4,3,2,1,0:T(8,128)(2,1)}), bf16[16,2,2,64,128]{4,3,2,1,0:T(8,128)(2,1)S(1)}, u32[]{:S(2)}, u32[]{:S(2)}) %all-to-all-start) | async-done | bytes 1048608 | tf_op jit(solution)/shard_map/keys_in/all_to_all | solution.py:378
  25.1 4.0 %all-to-all-start.1 = ((bf16[16,2,2,64,128]{4,3,2,1,0:T(8,128)(2,1)}), bf16[16,2,2,64,128]{4,3,2,1,0:T(8,128)(2,1)S(1)}, u32[]{:S(2)}, u32[]{:S(2)}) async-start(bf16[16,2,2,64,128]{4,3,2,1,0:T(8,128)(2,1)} %queries_in.1), calls=%async_computation.1 | async-start | bytes 2097152 | tf_op jit(solution)/shard_map/queries_in/all_to_all | solution.py:378
  29.1 0.5 halo.1
  29.5 6.3 %collective-permute-start = (bf16[2,896,128]{2,1,0:T(8,128)(2,1)S(1)}, bf16[2,896,128]{2,1,0:T(8,128)(2,1)S(1)}, u32[]{:S(2)}, u32[]{:S(2)}) collective-permute-start(bf16[2,896,128]{2,1,0:T(8,128)(2,1)S(1)} %halo.1), channel_id=1, source_target_pairs={{0,4},{4,8},{8,12},{12,16},{16,20},{20,24},{24,28},{28,32},{32,36}... | collective-permute-start | bytes 1376264 | tf_op jit(solution)/shard_map/halo/ppermute | solution.py:384
  35.8 5.4 %collective-permute-done.halo = bf16[2,896,128]{2,1,0:T(8,128)(2,1)S(1)} collective-permute-done((bf16[2,896,128]{2,1,0:T(8,128)(2,1)S(1)}, bf16[2,896,128]{2,1,0:T(8,128)(2,1)S(1)}, u32[]{:S(2)}, u32[]{:S(2)}) %collective-permute-start) | collective-permute-done | bytes 458784 | tf_op jit(solution)/shard_map/halo/ppermute | solution.py:384
  41.2 2.2 %all-to-all-done.1.moved = bf16[16,2,2,64,128]{4,3,2,1,0:T(8,128)(2,1)S(1)} async-done(((bf16[16,2,2,64,128]{4,3,2,1,0:T(8,128)(2,1)}), bf16[16,2,2,64,128]{4,3,2,1,0:T(8,128)(2,1)S(1)}, u32[]{:S(2)}, u32[]{:S(2)}) %all-to-all-start.1) | async-done | bytes 1048608 | tf_op jit(solution)/shard_map/queries_in/all_to_all | solution.py:378
  43.4 8.1 %attend.1 = (bf16[16,4,2,64,128]{4,3,2,1,0:T(8,128)(2,1)S(1)}, f32[2,2048,128]{2,1,0:T(8,128)S(1)}, bf16[2,768,128]{2,1,0:T(8,128)(2,1)S(1)}) custom-call(s32[1]{0:T(128)} %bitcast.first_group, bf16[16,2,2,64,128]{4,3,2,1,0:T(8,128)(2,1)S(1)} %all-to-all-done.1.moved, bf16[16,2,2,64,128]{4,3,2,1,0:T(8,128)(2,1)S(1)} %all-to-all-done.moved.moved_kv, ...), custom_call_target="tpu_custom_call" | custom-call | flops 3221225472 | bytes 8388608 | tf_op jit(solution)/shard_map/attend/pallas_call | solution.py:318
  51.5 5.6 %collective-permute-start.1 = (bf16[2,768,128]{2,1,0:T(8,128)(2,1)S(1)}, bf16[2,768,128]{2,1,0:T(8,128)(2,1)S(1)}, u32[]{:S(2)}, u32[]{:S(2)}) collective-permute-start(bf16[2,768,128]{2,1,0:T(8,128)(2,1)S(1)} %get-tuple-element.12), channel_id=1, source_target_pairs={{4,0},{8,4},{12,8},{16,12},{20,16},{24,20},{28,24},{32,28},{36,32}... | collective-permute-start | bytes 1179656 | tf_op jit(solution)/shard_map/halo_back/ppermute | solution.py:384
  57.2 7.0 %collective-permute-done.1.back = bf16[2,768,128]{2,1,0:T(8,128)(2,1)S(1)} collective-permute-done((bf16[2,768,128]{2,1,0:T(8,128)(2,1)S(1)}, bf16[2,768,128]{2,1,0:T(8,128)(2,1)S(1)}, u32[]{:S(2)}, u32[]{:S(2)}) %collective-permute-start.1) | collective-permute-done | bytes 393248 | tf_op jit(solution)/shard_map/halo_back/ppermute | solution.py:384
  64.1 0.6 halo_back.1
  64.7 30.8 %all_to_all.15.moved = bf16[16,4,2,64,128]{4,3,2,1,0:T(8,128)(2,1)S(1)} all-to-all(bf16[16,4,2,64,128]{4,3,2,1,0:T(8,128)(2,1)S(1)} %halo_back.1), channel_id=1, replica_groups=mesh['head'=4,'seq'=16,'ctx'=4] {'ctx','head'}, dimensions={0} | all-to-all | bytes 4194304 | tf_op jit(solution)/shard_map/outputs/all_to_all | solution.py:378
  95.5 1.5 %outputs.1 = (bf16[2,64,2048]{2,1,0:T(8,128)(2,1)}, bf16[2,64,2048]{2,1,0:T(8,128)(2,1)}, bf16[2,64,2048]{2,1,0:T(8,128)(2,1)}, bf16[2,64,2048]{2,1,0:T(8,128)(2,1)}) custom-call(bf16[16,4,2,64,128]{4,3,2,1,0:T(8,128)(2,1)S(1)} %all_to_all.15.moved), custom_call_target="tpu_custom_call" | custom-call | bytes 4194304 | tf_op jit(solution)/shard_map/outputs/pallas_call | solution.py:93
Async XLA Ops:
  2.8 22.3 %all-to-all-start = ((bf16[16,2,2,64,128]{4,3,2,1,0:T(8,128)(2,1)}), bf16[16,2,2,64,128]{4,3,2,1,0:T(8,128)(2,1)S(1)}, u32[]{:S(2)}, u32[]{:S(2)}) async-start(bf16[16,2,2,64,128]{4,3,2,1,0:T(8,128)(2,1)} %keys_in.1), calls=%async_computation | async-start | bytes 2097152 | tf_op jit(solution)/shard_map/keys_in/all_to_all | solution.py:378
  25.1 18.3 %all-to-all-start.1 = ((bf16[16,2,2,64,128]{4,3,2,1,0:T(8,128)(2,1)}), bf16[16,2,2,64,128]{4,3,2,1,0:T(8,128)(2,1)S(1)}, u32[]{:S(2)}, u32[]{:S(2)}) async-start(bf16[16,2,2,64,128]{4,3,2,1,0:T(8,128)(2,1)} %queries_in.1), calls=%async_computation.1 | async-start | bytes 2097152 | tf_op jit(solution)/shard_map/queries_in/all_to_all | solution.py:378
  29.5 11.7 %collective-permute-start = (bf16[2,896,128]{2,1,0:T(8,128)(2,1)S(1)}, bf16[2,896,128]{2,1,0:T(8,128)(2,1)S(1)}, u32[]{:S(2)}, u32[]{:S(2)}) collective-permute-start(bf16[2,896,128]{2,1,0:T(8,128)(2,1)S(1)} %halo.1), channel_id=1, source_target_pairs={{0,4},{4,8},{8,12},{12,16},{16,20},{20,24},{24,28},{28,32},{32,36}... | collective-permute-start | bytes 1376264 | tf_op jit(solution)/shard_map/halo/ppermute | solution.py:384
  51.5 12.6 %collective-permute-start.1 = (bf16[2,768,128]{2,1,0:T(8,128)(2,1)S(1)}, bf16[2,768,128]{2,1,0:T(8,128)(2,1)S(1)}, u32[]{:S(2)}, u32[]{:S(2)}) collective-permute-start(bf16[2,768,128]{2,1,0:T(8,128)(2,1)S(1)} %get-tuple-element.12), channel_id=1, source_target_pairs={{4,0},{8,4},{12,8},{16,12},{20,16},{24,20},{28,24},{32,28},{36,32}... | collective-permute-start | bytes 1179656 | tf_op jit(solution)/shard_map/halo_back/ppermute | solution.py:384

commit v7 on v6

--- a/solution.py
+++ b/solution.py
@@ -80,19 +80,21 @@
 
 
 def join_body(moved, *outs):
-    block = pl.program_id(0)
+    block, part = pl.program_id(0), pl.program_id(1)
+    rows = outs[0].shape[1]
+    at = pl.ds(pl.multiple_of(part * rows, rows), rows)
     for which, out in enumerate(outs):
         for head in range(moved.shape[0]):
-            out[0, :, head * HD : (head + 1) * HD] = moved[head, which, block]
+            out[0, :, head * HD : (head + 1) * HD] = moved[head, which, block, at]
 
 
 def join(moved):
     heads, count, blocks, rows, _ = moved.shape
     out = jax.ShapeDtypeStruct((blocks, rows, heads * HD), moved.dtype)
-    one = pl.BlockSpec((1, rows, heads * HD), lambda block: (block, 0, 0))
+    one = pl.BlockSpec((1, rows // 2, heads * HD), lambda block, part: (block, part, 0))
     return pl.pallas_call(
         join_body,
-        grid=(blocks,),
+        grid=(blocks, 2),
         out_shape=(out,) * count,
         in_specs=whole(1),
         out_specs=(one,) * count,

time: 97.4 us -> 97.8 us (level)
  no operation moved by 1% of the time
where the time goes in v7:
time: 97.8 us; the launch traced here: 97.4 us
  blocking collectives  30.8 us (31%)
  waiting for transfers between devices  28 us (29%)
  starting transfers between devices  22.6 us (23%)
  Pallas kernels  15.4 us (16%)
    all_to_all x1, blocking collectives, exchange(): lax.all_to_all(parts, GROUP_AXES, split_axis=0, concat_axis=0, tiled=True)  30.8 us
    all_to_all x2, waiting for transfers between devices, exchange(): lax.all_to_all(parts, GROUP_AXES, split_axis=0, concat_axis=0, tiled=True)  15.6 us
    ppermute x2, waiting for transfers between devices, shifted(): return lax.ppermute(block, 'seq', route)  12.4 us
    ppermute x2, starting transfers between devices, shifted(): return lax.ppermute(block, 'seq', route)  11.9 us
    all_to_all x2, starting transfers between devices, exchange(): lax.all_to_all(parts, GROUP_AXES, split_axis=0, concat_axis=0, tiled=True)  10.7 us
    pallas_call x1, Pallas kernels, attend(): pl.pallas_call(attend_body, out_shape=(jax.ShapeDtypeStruct((moved.shape[...  8.13 us
    pallas_call x2, Pallas kernels, spread(): pl.pallas_call(spread_body, out_shape=jax.ShapeDtypeStruct((heads, count,...  4.29 us
  transfers between devices with their start and end apart: 4, of which 4 were waited for; matrix products, arithmetic and copies ran while one was open for 0% of the time, Pallas kernels for 3%

profile of v7, /device:TPU:33, one launch (start us, length us, event | category | flops | bytes accessed | tf_op | source)
XLA Modules:
  0.0 97.4 jit_solution(11511167853426811352)
XLA Ops:
  0.6 2.2 %keys_in.1 = bf16[16,2,2,64,128]{4,3,2,1,0:T(8,128)(2,1)} custom-call(bf16[2,64,2048]{2,1,0:T(8,128)(2,1)} %refs_0_.3, bf16[2,64,2048]{2,1,0:T(8,128)(2,1)} %refs_1_.3), custom_call_target="tpu_custom_call" | custom-call | bytes 2097152 | tf_op jit(solution)/shard_map/keys_in/pallas_call | solution.py:69
  2.8 6.8 %all-to-all-start = ((bf16[16,2,2,64,128]{4,3,2,1,0:T(8,128)(2,1)}), bf16[16,2,2,64,128]{4,3,2,1,0:T(8,128)(2,1)S(1)}, u32[]{:S(2)}, u32[]{:S(2)}) async-start(bf16[16,2,2,64,128]{4,3,2,1,0:T(8,128)(2,1)} %keys_in.1), calls=%async_computation | async-start | bytes 2097152 | tf_op jit(solution)/shard_map/keys_in/all_to_all | solution.py:380
  9.6 2.1 %queries_in.1 = bf16[16,2,2,64,128]{4,3,2,1,0:T(8,128)(2,1)} custom-call(bf16[2,64,2048]{2,1,0:T(8,128)(2,1)} %refs_0_.2, bf16[2,64,2048]{2,1,0:T(8,128)(2,1)} %refs_1_.2), custom_call_target="tpu_custom_call" | custom-call | bytes 2097152 | tf_op jit(solution)/shard_map/queries_in/pallas_call | solution.py:69
  11.7 13.4 %all-to-all-done.moved.moved_kv = bf16[16,2,2,64,128]{4,3,2,1,0:T(8,128)(2,1)S(1)} async-done(((bf16[16,2,2,64,128]{4,3,2,1,0:T(8,128)(2,1)}), bf16[16,2,2,64,128]{4,3,2,1,0:T(8,128)(2,1)S(1)}, u32[]{:S(2)}, u32[]{:S(2)}) %all-to-all-start) | async-done | bytes 1048608 | tf_op jit(solution)/shard_map/keys_in/all_to_all | solution.py:380
  25.1 4.0 %all-to-all-start.1 = ((bf16[16,2,2,64,128]{4,3,2,1,0:T(8,128)(2,1)}), bf16[16,2,2,64,128]{4,3,2,1,0:T(8,128)(2,1)S(1)}, u32[]{:S(2)}, u32[]{:S(2)}) async-start(bf16[16,2,2,64,128]{4,3,2,1,0:T(8,128)(2,1)} %queries_in.1), calls=%async_computation.1 | async-start | bytes 2097152 | tf_op jit(solution)/shard_map/queries_in/all_to_all | solution.py:380
  29.1 0.5 halo.1
  29.5 6.3 %collective-permute-start = (bf16[2,896,128]{2,1,0:T(8,128)(2,1)S(1)}, bf16[2,896,128]{2,1,0:T(8,128)(2,1)S(1)}, u32[]{:S(2)}, u32[]{:S(2)}) collective-permute-start(bf16[2,896,128]{2,1,0:T(8,128)(2,1)S(1)} %halo.1), channel_id=1, source_target_pairs={{0,4},{4,8},{8,12},{12,16},{16,20},{20,24},{24,28},{28,32},{32,36}... | collective-permute-start | bytes 1376264 | tf_op jit(solution)/shard_map/halo/ppermute | solution.py:386
  35.8 5.4 %collective-permute-done.halo = bf16[2,896,128]{2,1,0:T(8,128)(2,1)S(1)} collective-permute-done((bf16[2,896,128]{2,1,0:T(8,128)(2,1)S(1)}, bf16[2,896,128]{2,1,0:T(8,128)(2,1)S(1)}, u32[]{:S(2)}, u32[]{:S(2)}) %collective-permute-start) | collective-permute-done | bytes 458784 | tf_op jit(solution)/shard_map/halo/ppermute | solution.py:386
  41.2 2.2 %all-to-all-done.1.moved = bf16[16,2,2,64,128]{4,3,2,1,0:T(8,128)(2,1)S(1)} async-done(((bf16[16,2,2,64,128]{4,3,2,1,0:T(8,128)(2,1)}), bf16[16,2,2,64,128]{4,3,2,1,0:T(8,128)(2,1)S(1)}, u32[]{:S(2)}, u32[]{:S(2)}) %all-to-all-start.1) | async-done | bytes 1048608 | tf_op jit(solution)/shard_map/queries_in/all_to_all | solution.py:380
  43.4 8.1 %attend.1 = (bf16[16,4,2,64,128]{4,3,2,1,0:T(8,128)(2,1)S(1)}, f32[2,2048,128]{2,1,0:T(8,128)S(1)}, bf16[2,768,128]{2,1,0:T(8,128)(2,1)S(1)}) custom-call(s32[1]{0:T(128)} %bitcast.first_group, bf16[16,2,2,64,128]{4,3,2,1,0:T(8,128)(2,1)S(1)} %all-to-all-done.1.moved, bf16[16,2,2,64,128]{4,3,2,1,0:T(8,128)(2,1)S(1)} %all-to-all-done.moved.moved_kv, ...), custom_call_target="tpu_custom_call" | custom-call | flops 3221225472 | bytes 8388608 | tf_op jit(solution)/shard_map/attend/pallas_call | solution.py:320
  51.5 5.6 %collective-permute-start.1 = (bf16[2,768,128]{2,1,0:T(8,128)(2,1)S(1)}, bf16[2,768,128]{2,1,0:T(8,128)(2,1)S(1)}, u32[]{:S(2)}, u32[]{:S(2)}) collective-permute-start(bf16[2,768,128]{2,1,0:T(8,128)(2,1)S(1)} %get-tuple-element.12), channel_id=1, source_target_pairs={{4,0},{8,4},{12,8},{16,12},{20,16},{24,20},{28,24},{32,28},{36,32}... | collective-permute-start | bytes 1179656 | tf_op jit(solution)/shard_map/halo_back/ppermute | solution.py:386
  57.2 7.0 %collective-permute-done.1.back = bf16[2,768,128]{2,1,0:T(8,128)(2,1)S(1)} collective-permute-done((bf16[2,768,128]{2,1,0:T(8,128)(2,1)S(1)}, bf16[2,768,128]{2,1,0:T(8,128)(2,1)S(1)}, u32[]{:S(2)}, u32[]{:S(2)}) %collective-permute-start.1) | collective-permute-done | bytes 393248 | tf_op jit(solution)/shard_map/halo_back/ppermute | solution.py:386
  64.1 0.6 halo_back.1
  64.7 30.8 %all_to_all.15.moved = bf16[16,4,2,64,128]{4,3,2,1,0:T(8,128)(2,1)S(1)} all-to-all(bf16[16,4,2,64,128]{4,3,2,1,0:T(8,128)(2,1)S(1)} %halo_back.1), channel_id=1, replica_groups=mesh['head'=4,'seq'=16,'ctx'=4] {'ctx','head'}, dimensions={0} | all-to-all | bytes 4194304 | tf_op jit(solution)/shard_map/outputs/all_to_all | solution.py:380
  95.5 1.9 %outputs.1 = (bf16[2,64,2048]{2,1,0:T(8,128)(2,1)}, bf16[2,64,2048]{2,1,0:T(8,128)(2,1)}, bf16[2,64,2048]{2,1,0:T(8,128)(2,1)}, bf16[2,64,2048]{2,1,0:T(8,128)(2,1)}) custom-call(bf16[16,4,2,64,128]{4,3,2,1,0:T(8,128)(2,1)S(1)} %all_to_all.15.moved), custom_call_target="tpu_custom_call" | custom-call | bytes 4194304 | tf_op jit(solution)/shard_map/outputs/pallas_call | solution.py:95
Async XLA Ops:
  2.8 22.3 %all-to-all-start = ((bf16[16,2,2,64,128]{4,3,2,1,0:T(8,128)(2,1)}), bf16[16,2,2,64,128]{4,3,2,1,0:T(8,128)(2,1)S(1)}, u32[]{:S(2)}, u32[]{:S(2)}) async-start(bf16[16,2,2,64,128]{4,3,2,1,0:T(8,128)(2,1)} %keys_in.1), calls=%async_computation | async-start | bytes 2097152 | tf_op jit(solution)/shard_map/keys_in/all_to_all | solution.py:380
  25.1 18.3 %all-to-all-start.1 = ((bf16[16,2,2,64,128]{4,3,2,1,0:T(8,128)(2,1)}), bf16[16,2,2,64,128]{4,3,2,1,0:T(8,128)(2,1)S(1)}, u32[]{:S(2)}, u32[]{:S(2)}) async-start(bf16[16,2,2,64,128]{4,3,2,1,0:T(8,128)(2,1)} %queries_in.1), calls=%async_computation.1 | async-start | bytes 2097152 | tf_op jit(solution)/shard_map/queries_in/all_to_all | solution.py:380
  29.5 11.7 %collective-permute-start = (bf16[2,896,128]{2,1,0:T(8,128)(2,1)S(1)}, bf16[2,896,128]{2,1,0:T(8,128)(2,1)S(1)}, u32[]{:S(2)}, u32[]{:S(2)}) collective-permute-start(bf16[2,896,128]{2,1,0:T(8,128)(2,1)S(1)} %halo.1), channel_id=1, source_target_pairs={{0,4},{4,8},{8,12},{12,16},{16,20},{20,24},{24,28},{28,32},{32,36}... | collective-permute-start | bytes 1376264 | tf_op jit(solution)/shard_map/halo/ppermute | solution.py:386
  51.5 12.6 %collective-permute-start.1 = (bf16[2,768,128]{2,1,0:T(8,128)(2,1)S(1)}, bf16[2,768,128]{2,1,0:T(8,128)(2,1)S(1)}, u32[]{:S(2)}, u32[]{:S(2)}) collective-permute-start(bf16[2,768,128]{2,1,0:T(8,128)(2,1)S(1)} %get-tuple-element.12), channel_id=1, source_target_pairs={{4,0},{8,4},{12,8},{16,12},{20,16},{24,20},{28,24},{32,28},{36,32}... | collective-permute-start | bytes 1179656 | tf_op jit(solution)/shard_map/halo_back/ppermute | solution.py:386
